TPU v7x, 128 devices: a whole 4x4x4 slice. The times are simulated.
128 devices in a mesh: grp: 16 (over y, z_lo, core), sub: 8 (over x, z_hi).
Axes of the slice: x: 4, y: 4, z: 4 (z_hi: 2, z_lo: 2; z = z_hi * 2 + z_lo), core: 2. Of those that a mesh axis runs over, the one named last changes fastest.
Arguments:
- node_feats: bfloat16 [262144, 512], P(('grp', 'sub')), may hold values from -6 to 6
- node_grad: bfloat16 [262144, 512], P(('grp', 'sub')), may hold values from -6 to 6
- small_edges: bfloat16 [32768, 512], P(('grp', 'sub')), may hold values from -6 to 6
- giant_edges: bfloat16 [2048, 512], P(('grp', 'sub')), may hold values from -6 to 6
- pair_node: int32 [131072], P(('grp', 'sub')), may hold values from 0 to 262143, as said below
- pair_edge: int32 [131072], P(('grp', 'sub')), may hold values from 0 to 383
- send_count: int32 [128, 128], P(('grp', 'sub')), may hold values from 2 to 8, as said below
- w_in: bfloat16 [1024, 512], replicated, may hold values from -0.1875 to 0.1875
- b_in: float32 [512], replicated, may hold values from -4 to 4
- w_out: bfloat16 [512, 512], replicated, may hold values from -0.25 to 0.25
Outputs:
- grad_nodes: bfloat16 [262144, 512], P(('grp', 'sub'))
- grad_small: bfloat16 [32768, 512], P(('grp', 'sub'))
- grad_giant: bfloat16 [2048, 512], P(('grp', 'sub'))
- grad_w_in: float32 [1024, 512], replicated
- grad_b_in: float32 [512], replicated
- grad_w_out: float32 [512, 512], replicated
Inputs may be any that keep to these rules, and one draw needn't show every extreme that they name: `pair_node`: slots of bucket j on any device hold nodes owned by device j, ids j * 2048 to (j + 1) * 2048 - 1. `send_count`: no entry exceeds 8; in every draw some owner gets 8 live slots from every device.
All inputs are finite; a program needn't handle non-finite values.
Results may differ from a plain program's by a relative error of at most 0.017.
Values may be sent and summed in bfloat16 or wider, within the bound.
A program may use at most 128 MiB of HBM per device.

v0:
```python
import jax
import jax.numpy as jnp
from jax import lax
from jax.sharding import PartitionSpec as P


def move_index(values):
    return lax.all_to_all(values, ("grp", "sub"), split_axis=0, concat_axis=0, tiled=True)


def move_rows(values):
    return lax.all_to_all(values, ("grp", "sub"), split_axis=0, concat_axis=0, tiled=True)


def move_terms(values):
    return lax.all_to_all(values, ("grp", "sub"), split_axis=0, concat_axis=0, tiled=True)


def shards(
    node_feats,
    node_grad,
    small_edges,
    giant_edges,
    pair_node,
    pair_edge,
    send_count,
    w_in,
    b_in,
    w_out,
):
    grp_count = lax.axis_size("grp")
    sub_count = lax.axis_size("sub")
    devices = grp_count * sub_count
    pair_count = pair_node.shape[0]
    capacity = pair_count // devices
    node_dev = node_feats.shape[0]
    feat_width = node_feats.shape[1]
    small_count = small_edges.shape[0]
    giant_dev = giant_edges.shape[0]
    local_index = (pair_node % node_dev).reshape(devices, capacity)
    requested = move_index(local_index).reshape(pair_count)
    owner_table = jnp.concatenate([node_feats, node_grad], axis=1)
    served = jnp.take(owner_table, requested, axis=0).reshape(devices, capacity, 2 * feat_width)
    fetched = move_rows(served).reshape(pair_count, 2 * feat_width)
    positions = jnp.arange(pair_count, dtype=jnp.int32)
    live_slot = positions % capacity < send_count[0][positions // capacity]
    giant_group = lax.all_gather(giant_edges, "sub", axis=0, tiled=True)
    edge_table = jnp.concatenate([small_edges, giant_group], axis=0)
    joined = jnp.concatenate(
        [fetched[:, :feat_width], jnp.take(edge_table, pair_edge, axis=0)], axis=1
    )
    preact = jnp.dot(joined, w_in, preferred_element_type=jnp.float32) + b_in
    logistic = jax.nn.sigmoid(preact)
    hidden = (preact * logistic).astype(jnp.bfloat16)
    out_grad = jnp.where(live_slot[:, None], fetched[:, feat_width:], jnp.zeros((), jnp.bfloat16))
    grad_out = jnp.einsum("ph,pc->hc", hidden, out_grad, preferred_element_type=jnp.float32)
    hid_grad = jnp.einsum("pc,hc->ph", out_grad, w_out, preferred_element_type=jnp.float32)
    pre_grad = (hid_grad * logistic * (1.0 + preact * (1.0 - logistic))).astype(jnp.bfloat16)
    grad_in = jnp.einsum("pk,ph->kh", joined, pre_grad, preferred_element_type=jnp.float32)
    grad_bias = jnp.sum(pre_grad.astype(jnp.float32), axis=0)
    in_grad = jnp.einsum("ph,kh->pk", pre_grad, w_in, preferred_element_type=jnp.float32)
    node_term = in_grad[:, :feat_width].astype(jnp.bfloat16).reshape(devices, capacity, feat_width)
    edge_term = in_grad[:, feat_width:]
    returned = move_terms(node_term).reshape(pair_count, feat_width)
    node_sum = jax.ops.segment_sum(returned.astype(jnp.float32), requested, num_segments=node_dev)
    grad_nodes = (node_grad.astype(jnp.float32) + node_sum).astype(jnp.bfloat16)
    edge_sum = jax.ops.segment_sum(
        edge_term, pair_edge, num_segments=small_count + giant_group.shape[0]
    )
    grad_small = edge_sum[:small_count].astype(jnp.bfloat16)
    giant_part = edge_sum[small_count:]
    giant_total = lax.psum(giant_part.astype(jnp.bfloat16), "sub").astype(jnp.float32)
    giant_mine = lax.dynamic_slice_in_dim(
        giant_total, lax.axis_index("sub") * giant_dev, giant_dev, 0
    )
    grad_in, grad_bias, grad_out = lax.psum((grad_in, grad_bias, grad_out), ("grp", "sub"))
    return (grad_nodes, grad_small, giant_mine.astype(jnp.bfloat16), grad_in, grad_bias, grad_out)


def solution(mesh):
    placed = (
        P(("grp", "sub"), None),
        P(("grp", "sub"), None),
        P(("grp", "sub"), None),
        P(("grp", "sub"), None),
        P(("grp", "sub")),
        P(("grp", "sub")),
        P(("grp", "sub"), None),
        P(),
        P(),
        P(),
    )
    return jax.shard_map(
        shards,
        mesh=mesh,
        in_specs=placed,
        out_specs=(
            P(("grp", "sub"), None),
            P(("grp", "sub"), None),
            P(("grp", "sub"), None),
            P(),
            P(),
            P(),
        ),
        check_vma=False,
    )
```

profile of v0, /device:TPU:1, one launch (start us, length us, event | category | flops | bytes accessed | tf_op | source)
XLA Modules:
  0.0 382.6 jit_solution(15383830572174407962)
XLA Ops:
  7.2 0.0 copy-start
  7.2 0.8 add_select_fusion.1
  8.0 0.7 all_to_all.12
  8.7 11.5 %all-to-all-start = ((s32[128,1,8]{2,1,0:T(1,128)}), s32[128,1,8]{2,1,0:T(1,128)S(1)}, u32[]{:S(2)}, u32[]{:S(2)}) async-start(s32[128,1,8]{2,1,0:T(1,128)} %bitcast), calls=%async_computation | async-start | bytes 131072 | tf_op jit(solution)/shard_map/all_to_all | solution.py:8
  20.2 4.7 %pad_maximum_fusion = bf16[2048,1024]{1,0:T(8,128)(2,1)} fusion(bf16[2048,512]{1,0:T(8,128)(2,1)} %param.11, bf16[2048,512]{1,0:T(8,128)(2,1)} %param.10), kind=kLoop, calls=%fused_computation.5 | loop fusion | flops 8388608 | bytes 8388608 | tf_op jit(solution)/shard_map/concatenate | solution.py:42
  24.9 5.1 %all-to-all-done = s32[128,1,8]{2,1,0:T(1,128)S(1)} async-done(((s32[128,1,8]{2,1,0:T(1,128)}), s32[128,1,8]{2,1,0:T(1,128)S(1)}, u32[]{:S(2)}, u32[]{:S(2)}) %all-to-all-start) | async-done | bytes 4128 | tf_op jit(solution)/shard_map/all_to_all | solution.py:8
  30.0 0.0 copy-start.6
  30.0 0.1 broadcast_in_dim_reshape.3
  30.1 0.5 copy-done.6
  30.6 7.7 %gather_fusion.1 = bf16[1024,1024]{1,0:T(8,128)(2,1)S(1)} fusion(bf16[2048,1024]{1,0:T(8,128)(2,1)} %pad_maximum_fusion, s32[1024]{0:T(1024)S(1)} %broadcast_clamp_fusion), kind=kCustom, calls=%fused_computation.1 | custom fusion | bytes 4198400 | tf_op jit(solution)/shard_map/jit(_take)/gather | solution.py:43
  38.3 1.6 bitcast_select_fusion
  39.9 0.0 copy-start.1
  39.9 4.7 %all-to-all-start.1 = ((bf16[128,8,1024]{2,1,0:T(8,128)(2,1)}), bf16[128,8,1024]{2,1,0:T(8,128)(2,1)S(1)}, u32[]{:S(2)}, u32[]{:S(2)}) async-start(bf16[128,8,1024]{2,1,0:T(8,128)(2,1)} %bitcast_select_fusion), calls=%async_computation.1 | async-start | bytes 4194304 | tf_op jit(solution)/shard_map/all_to_all | solution.py:12
  44.6 0.0 all-reduce.4.cloned.1.call-start
  44.7 0.0 copy-done.1
  44.7 0.0 copy-start.8
  44.7 0.0 copy-start.9
  44.7 6.6 %gather_fusion = s32[1024]{0:T(1024)S(1)} fusion(s32[128]{0:T(128)S(1)} %bitcast.22, s32[1024]{0:T(1024)S(1)} %broadcast_clamp_fusion.1), kind=kCustom, calls=%fused_computation | custom fusion | bytes 12288 | tf_op jit(solution)/shard_map/gather | solution.py:46
  51.3 0.0 copy-done.8
  51.3 41.6 %all_gather.3 = bf16[128,512]{1,0:T(8,128)(2,1)S(1)} all-gather(bf16[16,512]{1,0:T(8,128)(2,1)S(1)} %copy-done.8), channel_id=1, replica_groups=mesh['grp'=16,'sub'=8] {'sub'}, dimensions={0}, use_global_device_ids=true | all-gather | bytes 147456 | tf_op jit(solution)/shard_map/all_gather | solution.py:47
  92.9 1.0 pad_maximum_fusion.4
  93.9 0.0 copy-done.9
  93.9 5.1 %gather_fusion.2 = bf16[1024,512]{1,0:T(8,128)(2,1)} fusion(bf16[384,512]{1,0:T(8,128)(2,1)S(1)} %pad_maximum_fusion.4, s32[1024]{0:T(1024)S(1)} %fusion.15), kind=kCustom, calls=%fused_computation.2 | custom fusion | bytes 2101248 | tf_op jit(solution)/shard_map/jit(_take)/gather | solution.py:50
  99.0 2.4 broadcast_select_fusion
  101.4 0.0 all-to-all-done.1
  101.4 0.1 slice.34
  101.5 0.0 copy-done
  101.5 1.1 copy-done.7
  102.6 1.2 fusion.5
  103.9 0.0 copy-done.4
  103.9 0.0 copy-done.11
  103.9 0.0 copy-start.10
  103.9 2.0 fusion.8
  105.9 0.0 copy-done.10
  105.9 1.7 convert_reduce_fusion
  107.6 0.0 copy-start.12
  107.6 1.0 copy-done.12
  108.6 3.2 fusion.21
  111.8 7.7 %scatter_custom_fusion.1 = f32[384,512]{1,0:T(8,128)S(1)} fusion(s32[1024]{0:T(1024)S(1)} %copy-done.9, f32[1024,1024]{1,0:T(8,128)} %fusion.21, f32[]{:T(128)} %constant.85.clone.1), kind=kCustom, calls=%fused_computation.6 | custom fusion | flops 524288 | bytes 2884096 | tf_op jit(solution)/shard_map/scatter-add | solution.py:67
  119.5 0.1 convert.9
  119.5 0.7 slice.38
  120.2 0.0 all-reduce.4.cloned.1.call-update
  120.2 0.0 all-reduce.6.cloned.1.call-start
  120.2 0.0 copy-done.5
  120.3 4.1 %fusion.4 = f32[1024,512]{1,0:T(8,128)} fusion(bf16[1024,512]{1,0:T(8,128)(2,1)} %copy-done.12, bf16[1024,512]{1,0:T(8,128)(2,1)} %broadcast_select_fusion, bf16[1024,512]{1,0:T(8,128)(2,1)S(1)} %copy-done.5), kind=kOutput, calls=%fused_computation.17 | convolution fusion | flops 1077936128 | bytes 5242880 | tf_op jit(solution)/shard_map/pk,ph->kh/dot_general | solution.py:59
  124.4 0.0 all-reduce.6.cloned.1.call-update
  124.4 0.0 copy-start.2
  124.4 2.8 fusion.6
  127.3 12.0 %all-to-all-start.2 = ((bf16[128,8,512]{2,1,0:T(8,128)(2,1)}), bf16[128,8,512]{2,1,0:T(8,128)(2,1)}, u32[]{:S(2)}, u32[]{:S(2)}) async-start(bf16[128,8,512]{2,1,0:T(8,128)(2,1)} %fusion.6), calls=%async_computation.2 | async-start | bytes 2097152 | tf_op jit(solution)/shard_map/all_to_all | solution.py:16
  139.3 0.0 copy-done.2
  139.3 2.5 convert_element_type.30
  141.8 0.5 broadcast.148
  142.3 1.6 reduce.5
  144.0 0.1 reshape.163
  144.1 0.7 slice.37
  144.8 68.5 %psum.30 = f32[512]{0:T(512)} all-reduce(f32[512]{0:T(512)S(1)} %get-tuple-element.8), channel_id=1, replica_groups=mesh['grp'=16,'sub'=8] {'grp','sub'}, use_global_device_ids=true, to_apply=%region_5.6 | all-reduce | flops 512 | bytes 4096 | tf_op jit(solution)/shard_map/psum | solution.py:76
  213.3 1.3 convert_convert_fusion
  214.6 0.0 all-to-all-done.2
  214.6 11.3 %scatter_custom_fusion = f32[2048,512]{1,0:T(8,128)} fusion(f32[2048,512]{1,0:T(8,128)} %convert_element_type.30, s32[1024]{0:T(1024)S(1)} %reshape.163, bf16[128,8,512]{2,1,0:T(8,128)(2,1)} %all-to-all-done.2), kind=kCustom, calls=%fused_computation.10 | custom fusion | flops 1048576 | bytes 5242880 | tf_op jit(solution)/shard_map/scatter-add | solution.py:65
  225.9 4.1 %convert_element_type.34 = bf16[2048,512]{1,0:T(8,128)(2,1)} convert(f32[2048,512]{1,0:T(8,128)} %scatter_custom_fusion) | non-fusion elementwise | flops 1048576 | bytes 6291456 | tf_op jit(solution)/shard_map/convert_element_type | solution.py:66
  230.0 141.7 %all-reduce.6.cloned.1.call-done = (f32[1024,512]{1,0:T(8,128)}, f32[512,512]{1,0:T(8,128)}) async-done(((f32[1024,512]{1,0:T(8,128)}, f32[512,512]{1,0:T(8,128)}), (f32[1024,512]{1,0:T(8,128)}, f32[512,512]{1,0:T(8,128)})) %all-reduce.6.cloned.1.call-update) | async-done | bytes 3145744 | tf_op jit(solution)/shard_map/psum | solution.py:76
  371.6 3.2 copy.21
  374.8 0.0 copy-done.3
  374.8 1.0 copy.22
  (14 shorter events, 0.1 us)
Async XLA Ops:
  7.2 94.3 %copy-start = (bf16[1024,512]{1,0:T(8,128)(2,1)S(1)}, bf16[1024,512]{1,0:T(8,128)(2,1)}, u32[]{:S(2)}) copy-start(bf16[1024,512]{1,0:T(8,128)(2,1)} %param.17) | copy-start | bytes 3145732
  8.7 21.3 %all-to-all-start = ((s32[128,1,8]{2,1,0:T(1,128)}), s32[128,1,8]{2,1,0:T(1,128)S(1)}, u32[]{:S(2)}, u32[]{:S(2)}) async-start(s32[128,1,8]{2,1,0:T(1,128)} %bitcast), calls=%async_computation | async-start | bytes 131072 | tf_op jit(solution)/shard_map/all_to_all | solution.py:8
  30.0 0.6 copy-start.6
  39.9 4.8 %copy-start.1 = (s32[1,128]{1,0:T(1,128)S(1)}, s32[1,128]{1,0:T(1,128)}, u32[]{:S(2)}) copy-start(s32[1,128]{1,0:T(1,128)} %param.16) | copy-start | bytes 1540
  39.9 61.5 %all-to-all-start.1 = ((bf16[128,8,1024]{2,1,0:T(8,128)(2,1)}), bf16[128,8,1024]{2,1,0:T(8,128)(2,1)S(1)}, u32[]{:S(2)}, u32[]{:S(2)}) async-start(bf16[128,8,1024]{2,1,0:T(8,128)(2,1)} %bitcast_select_fusion), calls=%async_computation.1 | async-start | bytes 4194304 | tf_op jit(solution)/shard_map/all_to_all | solution.py:12
  44.6 168.7 %all-reduce.4.cloned.1.call-start = ((), (), s32[]{:S(2)}) async-start(), calls=%async_computation.3 | async-start | bytes 262144 | tf_op jit(solution)/shard_map/psum | solution.py:72
  44.7 6.6 %copy-start.8 = (bf16[16,512]{1,0:T(8,128)(2,1)S(1)}, bf16[16,512]{1,0:T(8,128)(2,1)}, u32[]{:S(2)}) copy-start(bf16[16,512]{1,0:T(8,128)(2,1)} %param.13) | copy-start | bytes 49156
  44.7 49.1 %copy-start.9 = (s32[1024]{0:T(1024)S(1)}, s32[1024]{0:T(1024)}, u32[]{:S(2)}) copy-start(s32[1024]{0:T(1024)} %param.15) | copy-start | bytes 12292
  101.4 1.2 copy-start.7
  102.6 1.3 copy-start.4
  102.6 1.3 copy-start.11
  103.9 2.0 copy-start.10
  107.6 1.0 copy-start.12
  111.8 8.5 %copy-start.5 = (bf16[1024,512]{1,0:T(8,128)(2,1)S(1)}, bf16[1024,512]{1,0:T(8,128)(2,1)}, u32[]{:S(2)}) copy-start(bf16[1024,512]{1,0:T(8,128)(2,1)} %copy-done.4) | copy-start | bytes 3145732
  120.2 251.4 %all-reduce.6.cloned.1.call-start = ((), (), s32[]{:S(2)}) async-start(), calls=%async_computation.4 | async-start | bytes 6291456 | tf_op jit(solution)/shard_map/psum | solution.py:76
  124.4 14.8 %copy-start.2 = (bf16[2048,512]{1,0:T(8,128)(2,1)S(1)}, bf16[2048,512]{1,0:T(8,128)(2,1)}, u32[]{:S(2)}) copy-start(bf16[2048,512]{1,0:T(8,128)(2,1)} %param.11) | copy-start | bytes 6291460
  127.3 87.4 %all-to-all-start.2 = ((bf16[128,8,512]{2,1,0:T(8,128)(2,1)}), bf16[128,8,512]{2,1,0:T(8,128)(2,1)}, u32[]{:S(2)}, u32[]{:S(2)}) async-start(bf16[128,8,512]{2,1,0:T(8,128)(2,1)} %fusion.6), calls=%async_computation.2 | async-start | bytes 2097152 | tf_op jit(solution)/shard_map/all_to_all | solution.py:16
  371.6 3.2 copy-start.3
Sparse Core Ops, SparseCore 0:
  120.3 88.9 all-reduce.3
  215.4 156.1 all-reduce.5
where the time goes:
time: 383 us
  waiting for transfers between devices  147 us (38%)
  blocking collectives  110 us (29%)
  other arithmetic  39.1 us (10%)
  local copies, waits for them, and re-layouts  31.8 us (8%)
  starting transfers between devices  28.2 us (7%)
  between operations  14.3 us (4%)
  matrix products  12.3 us (3%)
    psum x1, waiting for transfers between devices, shards(): lax.psum((grad_in, grad_bias, grad_out), ('grp', 'sub'))  142 us
    psum x1, blocking collectives, shards(): lax.psum((grad_in, grad_bias, grad_out), ('grp', 'sub'))  68.5 us
    all_gather x1, blocking collectives, shards(): giant_group = lax.all_gather(giant_edges, 'sub', axis=0, tiled=True)  41.6 us
    all_to_all x1, starting transfers between devices, move_terms(): lax.all_to_all(values, ('grp', 'sub'), split_axis=0, concat_axis=0, tiled...  12 us
    all_to_all x1, starting transfers between devices, move_index(): lax.all_to_all(values, ('grp', 'sub'), split_axis=0, concat_axis=0, tiled...  11.5 us
    scatter-add x1, other arithmetic, shards(): jax.ops.segment_sum(returned.astype(jnp.float32), requested, num_segments...  11.3 us
    gather x1, local copies, waits for them, and re-layouts, shards(): jnp.take(owner_table, requested, axis=0)  7.7 us
  transfers between devices with their start and end apart: 5, of which 2 were waited for; matrix products, arithmetic and copies ran while one was open for 13% of the time, Pallas kernels for 0%

commit v1 on v0

--- a/solution.py
+++ b/solution.py
@@ -1,19 +1,74 @@
+import functools
+
 import jax
 import jax.numpy as jnp
 from jax import lax
+from jax.experimental import pallas as pl
+from jax.experimental.pallas import tpu as pltpu
 from jax.sharding import PartitionSpec as P
 
-
-def move_index(values):
-    return lax.all_to_all(values, ("grp", "sub"), split_axis=0, concat_axis=0, tiled=True)
+MESH = pl.DeviceIdType.MESH
 
 
-def move_rows(values):
-    return lax.all_to_all(values, ("grp", "sub"), split_axis=0, concat_axis=0, tiled=True)
+def mask_of(s):
+    core, par, y, x, zh = (s >> 6) & 1, (s >> 5) & 1, (s >> 3) & 3, (s >> 1) & 3, s & 1
+    zl = par ^ (x & 1) ^ (y & 1)
+    return (y << 5) | (zl << 4) | (core << 3) | (x << 1) | zh
 
 
-def move_terms(values):
-    return lax.all_to_all(values, ("grp", "sub"), split_axis=0, concat_axis=0, tiled=True)
+def place(j):
+    return (j // 8, lax.rem(j, 8))
+
+
+def exchange_kernel(count, x_ref, o_ref, send_sem, recv_sem):
+    me = lax.axis_index("grp") * 8 + lax.axis_index("sub")
+    barrier = pltpu.get_barrier_semaphore()
+
+    def greet(s, carry):
+        pl.semaphore_signal(barrier, inc=1, device_id=place(me ^ s), device_id_type=MESH)
+        return carry
+
+    lax.fori_loop(1, count, greet, 0)
+    pl.semaphore_wait(barrier, count - 1)
+
+    def send(s, carry):
+        j = me ^ mask_of(s)
+        pltpu.make_async_remote_copy(
+            src_ref=x_ref.at[j],
+            dst_ref=o_ref.at[me],
+            send_sem=send_sem,
+            recv_sem=recv_sem,
+            device_id=place(j),
+            device_id_type=MESH,
+        ).start()
+        return carry
+
+    lax.fori_loop(1, count, send, 0)
+    o_ref[me] = x_ref[me]
+    whole = pltpu.make_async_remote_copy(
+        src_ref=x_ref.at[pl.ds(1, count - 1)],
+        dst_ref=o_ref.at[pl.ds(1, count - 1)],
+        send_sem=send_sem,
+        recv_sem=recv_sem,
+        device_id=place(me ^ 1),
+        device_id_type=MESH,
+    )
+    whole.wait_recv()
+    whole.wait_send()
+
+
+def exchange(values, number):
+    count = values.shape[0]
+    return pl.pallas_call(
+        functools.partial(exchange_kernel, count),
+        out_shape=jax.ShapeDtypeStruct(values.shape, values.dtype),
+        in_specs=[pl.BlockSpec(memory_space=pltpu.VMEM)],
+        out_specs=pl.BlockSpec(memory_space=pltpu.VMEM),
+        scratch_shapes=[pltpu.SemaphoreType.DMA, pltpu.SemaphoreType.DMA],
+        compiler_params=pltpu.CompilerParams(
+            collective_id=number, has_side_effects=True, vmem_limit_bytes=32 << 20
+        ),
+    )(values)
 
 
 def shards(
@@ -38,10 +93,10 @@
     small_count = small_edges.shape[0]
     giant_dev = giant_edges.shape[0]
     local_index = (pair_node % node_dev).reshape(devices, capacity)
-    requested = move_index(local_index).reshape(pair_count)
+    requested = exchange(jnp.pad(local_index, ((0, 0), (0, 120))).reshape(devices, 1, 128), 1)[:, 0, :8].reshape(pair_count)
     owner_table = jnp.concatenate([node_feats, node_grad], axis=1)
     served = jnp.take(owner_table, requested, axis=0).reshape(devices, capacity, 2 * feat_width)
-    fetched = move_rows(served).reshape(pair_count, 2 * feat_width)
+    fetched = exchange(served, 2).reshape(pair_count, 2 * feat_width)
     positions = jnp.arange(pair_count, dtype=jnp.int32)
     live_slot = positions % capacity < send_count[0][positions // capacity]
     giant_group = lax.all_gather(giant_edges, "sub", axis=0, tiled=True)
@@ -61,7 +116,7 @@
     in_grad = jnp.einsum("ph,kh->pk", pre_grad, w_in, preferred_element_type=jnp.float32)
     node_term = in_grad[:, :feat_width].astype(jnp.bfloat16).reshape(devices, capacity, feat_width)
     edge_term = in_grad[:, feat_width:]
-    returned = move_terms(node_term).reshape(pair_count, feat_width)
+    returned = exchange(node_term, 3).reshape(pair_count, feat_width)
     node_sum = jax.ops.segment_sum(returned.astype(jnp.float32), requested, num_segments=node_dev)
     grad_nodes = (node_grad.astype(jnp.float32) + node_sum).astype(jnp.bfloat16)
     edge_sum = jax.ops.segment_sum(

time: 383 us -> 398 us (1.039)
  Pallas kernels: 0 us -> 81.1 us
  starting transfers between devices: 28.2 us -> 0.26 us
  waiting for transfers between devices: 147 us -> 127 us
  blocking collectives: 110 us -> 94.7 us
    pallas_call x0 -> x3, Pallas kernels: none -> 81.1 us  [exchange(): pl.pallas_call(functools.partial(exchange_kernel, count), out_shape=jax.S...]
    all_to_all x3 -> x0, starting transfers between devices: 28.2 us -> none  [the longest x1 12 us: move_terms(): lax.all_to_all(values, ('grp', 'sub'), split_axis=0, concat_axis=0, tiled...]
    psum x1, waiting for transfers between devices: 142 us -> 127 us  [shards(): lax.psum((grad_in, grad_bias, grad_out), ('grp', 'sub'))]
    all_gather x1, blocking collectives: 41.6 us -> 29.9 us  [shards(): giant_group = lax.all_gather(giant_edges, 'sub', axis=0, tiled=True)]
    all_to_all x3 -> x0, waiting for transfers between devices: 5.08 us -> none  [the longest x1 5.08 us: move_index(): lax.all_to_all(values, ('grp', 'sub'), split_axis=0, concat_axis=0, tiled...]
  transfers between devices with their start and end apart: 5 -> 2, of which waited for: 2 -> 1; matrix products, arithmetic and copies ran while one was open for 13% -> 7% of each run, Pallas kernels for 0% -> 6%
where the time goes in v1:
time: 398 us; the launch traced here: 397 us
  waiting for transfers between devices  127 us (32%)
  blocking collectives  94.7 us (24%)
  Pallas kernels  81.1 us (20%)
  other arithmetic  36.2 us (9%)
  local copies, waits for them, and re-layouts  30.9 us (8%)
  between operations  14.3 us (4%)
  matrix products  12.5 us (3%)
    psum x1, waiting for transfers between devices, shards(): lax.psum((grad_in, grad_bias, grad_out), ('grp', 'sub'))  127 us
    pallas_call x3, Pallas kernels, exchange(): pl.pallas_call(functools.partial(exchange_kernel, count), out_shape=jax.S...  81.1 us
    psum x1, blocking collectives, shards(): lax.psum((grad_in, grad_bias, grad_out), ('grp', 'sub'))  64.9 us
    all_gather x1, blocking collectives, shards(): giant_group = lax.all_gather(giant_edges, 'sub', axis=0, tiled=True)  29.9 us
    scatter-add x1, other arithmetic, shards(): jax.ops.segment_sum(returned.astype(jnp.float32), requested, num_segments...  10.9 us
    scatter-add x1, other arithmetic, shards(): jax.ops.segment_sum(edge_term, pair_edge, num_segments=small_count + gian...  8.29 us
  transfers between devices with their start and end apart: 2, of which 1 were waited for; matrix products, arithmetic and copies ran while one was open for 7% of the time, Pallas kernels for 6%

profile of v1, /device:TPU:1, one launch (start us, length us, event | category | flops | bytes accessed | tf_op | source)
XLA Modules:
  0.0 397.0 jit_solution(550335688037741408)
XLA Ops:
  7.2 0.0 copy-start
  7.2 0.0 copy-start.1
  7.2 0.0 all-reduce.5.cloned.1.call-start
  7.2 0.8 compare_and_fusion.1
  8.0 0.7 fusion.15
  8.7 0.7 add_select_fusion.1
  9.4 0.1 reshape.129
  9.5 18.1 %shard_map.145 = s32[128,1,128]{2,1,0:T(1,128)S(1)} custom-call(s32[128,1,128]{2,1,0:T(1,128)S(1)} %bitcast.25), custom_call_target="tpu_custom_call" | custom-call | tf_op jit(solution)/shard_map/pallas_call | solution.py:62
  27.7 0.8 fusion.21
  28.5 0.1 broadcast_in_dim_reshape_squeeze.3
  28.6 0.0 copy-done.1
  28.6 0.0 copy-start.12
  28.6 0.0 copy-start.2
  28.7 6.6 %gather_fusion = s32[1024]{0:T(1024)S(1)} fusion(s32[128]{0:T(128)S(1)} %bitcast.26, s32[1024]{0:T(1024)S(1)} %broadcast_clamp_fusion.1), kind=kCustom, calls=%fused_computation | custom fusion | bytes 12288 | tf_op jit(solution)/shard_map/gather | solution.py:101
  35.3 0.0 copy-done.12
  35.3 29.9 %all_gather.3 = bf16[128,512]{1,0:T(8,128)(2,1)} all-gather(bf16[16,512]{1,0:T(8,128)(2,1)S(1)} %copy-done.12), channel_id=1, replica_groups=mesh['grp'=16,'sub'=8] {'sub'}, dimensions={0}, use_global_device_ids=true | all-gather | bytes 147456 | tf_op jit(solution)/shard_map/all_gather | solution.py:102
  65.2 0.0 copy-done.2
  65.2 4.1 %pad_maximum_fusion = bf16[2048,1024]{1,0:T(8,128)(2,1)} fusion(bf16[2048,512]{1,0:T(8,128)(2,1)S(1)} %copy-done.2, bf16[2048,512]{1,0:T(8,128)(2,1)} %param.10), kind=kLoop, calls=%fused_computation.5 | loop fusion | flops 8388608 | bytes 8388608 | tf_op jit(solution)/shard_map/concatenate | solution.py:97
  69.3 7.7 %gather_fusion.1 = bf16[1024,1024]{1,0:T(8,128)(2,1)S(1)} fusion(bf16[2048,1024]{1,0:T(8,128)(2,1)} %pad_maximum_fusion, s32[1024]{0:T(1024)S(1)} %broadcast_clamp_fusion), kind=kCustom, calls=%fused_computation.1 | custom fusion | bytes 4198400 | tf_op jit(solution)/shard_map/jit(_take)/gather | solution.py:98
  77.0 0.3 bitcast_select_fusion.x_ref
  77.3 40.4 %shard_map.146 = bf16[128,8,1024]{2,1,0:T(8,128)(2,1)S(1)} custom-call(bf16[128,8,1024]{2,1,0:T(8,128)(2,1)S(1)} %bitcast_select_fusion.x_ref), custom_call_target="tpu_custom_call" | custom-call | tf_op jit(solution)/shard_map/pallas_call | solution.py:62
  117.7 0.0 copy-start.9
  117.7 0.0 copy-start.10
  117.7 1.1 slice.38
  118.8 0.0 copy-done.9
  118.8 0.0 copy-done.10
  118.8 5.1 %gather_fusion.2 = bf16[1024,512]{1,0:T(8,128)(2,1)} fusion(bf16[384,512]{1,0:T(8,128)(2,1)S(1)} %pad_maximum_fusion.4, s32[1024]{0:T(1024)S(1)} %fusion.15), kind=kCustom, calls=%fused_computation.2 | custom fusion | bytes 2101248 | tf_op jit(solution)/shard_map/jit(_take)/gather | solution.py:105
  123.9 1.5 broadcast_select_fusion
  125.4 0.0 copy-done
  125.5 0.0 copy-done.5
  125.5 0.0 copy-start.7
  125.5 0.0 copy-start.13
  125.5 0.0 copy-start.14
  125.5 1.2 fusion.5
  126.8 0.1 copy-done.13
  126.9 1.7 convert_reduce_fusion
  128.6 0.0 copy-start.15
  128.6 1.0 copy-done.15
  129.6 3.2 fusion.22
  132.8 8.3 %scatter_custom_fusion.1 = f32[384,512]{1,0:T(8,128)} fusion(s32[1024]{0:T(1024)} %param.15, f32[1024,1024]{1,0:T(8,128)} %fusion.22, f32[]{:T(128)} %constant.85.clone.1), kind=kCustom, calls=%fused_computation.6 | custom fusion | flops 524288 | bytes 2884096 | tf_op jit(solution)/shard_map/scatter-add | solution.py:122
  141.1 1.2 convert.9
  142.3 0.7 slice.42
  142.9 0.0 all-reduce.5.cloned.1.call-update
  143.0 0.2 all-reduce.7.cloned.1.call-start
  143.2 0.0 copy-start.6
  143.2 0.0 copy-start.16
  143.2 3.7 fusion.8
  146.9 2.6 fusion.4
  149.5 0.0 all-reduce.7.cloned.1.call-update
  149.6 0.7 slice.41
  150.3 0.9 copy-done.3
  151.2 2.6 convert_element_type.30
  153.8 0.0 copy-done.11
  153.8 0.1 reshape.160
  153.9 1.7 fusion.6.x_ref
  155.6 22.6 %shard_map.147 = bf16[128,8,512]{2,1,0:T(8,128)(2,1)S(1)} custom-call(bf16[128,8,512]{2,1,0:T(8,128)(2,1)S(1)} %fusion.6.x_ref), custom_call_target="tpu_custom_call" | custom-call | tf_op jit(solution)/shard_map/pallas_call | solution.py:62
  178.2 10.9 %scatter_custom_fusion = f32[2048,512]{1,0:T(8,128)} fusion(f32[2048,512]{1,0:T(8,128)} %convert_element_type.30, s32[1024]{0:T(1024)S(1)} %reshape.160, bf16[128,8,512]{2,1,0:T(8,128)(2,1)S(1)} %shard_map.147), kind=kCustom, calls=%fused_computation.10 | custom fusion | flops 1048576 | bytes 5242880 | tf_op jit(solution)/shard_map/scatter-add | solution.py:120
  189.1 3.8 convert_element_type.34
  192.8 64.9 %psum.30 = f32[512]{0:T(512)} all-reduce(f32[512]{0:T(512)S(1)} %get-tuple-element.10), channel_id=1, replica_groups=mesh['grp'=16,'sub'=8] {'grp','sub'}, use_global_device_ids=true, to_apply=%region_5.6 | all-reduce | flops 512 | bytes 4096 | tf_op jit(solution)/shard_map/psum | solution.py:131
  257.7 1.3 convert_convert_fusion
  259.0 127.0 %all-reduce.7.cloned.1.call-done = (f32[1024,512]{1,0:T(8,128)}, f32[512,512]{1,0:T(8,128)}) async-done(((f32[1024,512]{1,0:T(8,128)}, f32[512,512]{1,0:T(8,128)}), (f32[1024,512]{1,0:T(8,128)}, f32[512,512]{1,0:T(8,128)})) %all-reduce.7.cloned.1.call-update) | async-done | bytes 3145744 | tf_op jit(solution)/shard_map/psum | solution.py:131
  386.0 3.2 copy.20
  389.1 0.0 copy-done.4
  389.1 1.0 copy.21
  (21 shorter events, 0.1 us)
Async XLA Ops:
  7.2 118.3 %copy-start = (bf16[1024,512]{1,0:T(8,128)(2,1)S(1)}, bf16[1024,512]{1,0:T(8,128)(2,1)}, u32[]{:S(2)}) copy-start(bf16[1024,512]{1,0:T(8,128)(2,1)} %param.17) | copy-start | bytes 3145732
  7.2 21.4 %copy-start.1 = (s32[1,128]{1,0:T(1,128)S(1)}, s32[1,128]{1,0:T(1,128)}, u32[]{:S(2)}) copy-start(s32[1,128]{1,0:T(1,128)} %param.16) | copy-start | bytes 1540
  7.2 250.5 %all-reduce.5.cloned.1.call-start = ((), (), s32[]{:S(2)}) async-start(), calls=%async_computation | async-start | bytes 262144 | tf_op jit(solution)/shard_map/psum | solution.py:127
  28.6 6.6 %copy-start.12 = (bf16[16,512]{1,0:T(8,128)(2,1)S(1)}, bf16[16,512]{1,0:T(8,128)(2,1)}, u32[]{:S(2)}) copy-start(bf16[16,512]{1,0:T(8,128)(2,1)} %param.13) | copy-start | bytes 49156
  28.6 36.5 %copy-start.2 = (bf16[2048,512]{1,0:T(8,128)(2,1)S(1)}, bf16[2048,512]{1,0:T(8,128)(2,1)}, u32[]{:S(2)}) copy-start(bf16[2048,512]{1,0:T(8,128)(2,1)} %param.11) | copy-start | bytes 6291460
  117.7 1.1 copy-start.9
  117.7 1.1 copy-start.10
  123.9 1.5 copy-start.5
  125.5 1.3 copy-start.7
  125.5 1.4 copy-start.13
  125.5 1.4 copy-start.14
  126.9 1.7 copy-start.17
  128.6 1.0 copy-start.15
  143.0 243.0 %all-reduce.7.cloned.1.call-start = ((), (), s32[]{:S(2)}) async-start(), calls=%async_computation.1 | async-start | bytes 6291456 | tf_op jit(solution)/shard_map/psum | solution.py:131
  143.2 3.7 copy-start.6
  143.2 3.7 copy-start.8
  143.2 3.7 copy-start.16
  149.5 1.7 copy-start.3
  151.2 2.6 copy-start.11
  386.0 3.2 copy-start.4
Sparse Core Ops, SparseCore 0:
  143.1 80.2 all-reduce.4
  229.5 156.3 all-reduce.6

commit v2 on v0

v2 whole, which is shorter than its diff:
```python
import functools

import jax
import jax.numpy as jnp
from jax import lax
from jax.experimental import pallas as pl
from jax.experimental.pallas import tpu as pltpu
from jax.sharding import PartitionSpec as P

MESH = pl.DeviceIdType.MESH
BF = jnp.bfloat16
F32 = jnp.float32
I32 = jnp.int32
DEVICES = 128
SUB = 8
GRP = 16
CAP = 8
SLOTS = 1024
WIDTH = 512
NODES = 2048
SMALL = 256
GIANT = 16
EDGES = SMALL + GIANT * SUB
CHUNKS = 4
PER = DEVICES // CHUNKS
ROWS = PER * CAP


def device_of(x, y, z, core):
    return (y * 4 + (z & 1) * 2 + core, x * 2 + (z >> 1))


def mask_of(s):
    core, par, y, x, zh = (s >> 6) & 1, (s >> 5) & 1, (s >> 3) & 3, (s >> 1) & 3, s & 1
    zl = par ^ (x & 1) ^ (y & 1)
    return (y << 5) | (zl << 4) | (core << 3) | (x << 1) | zh


def place(j):
    return (j // SUB, lax.rem(j, SUB))


def dot(a, b, ca=1, cb=0):
    return lax.dot_general(
        a, b, (((ca,), (cb,)), ((), ())), preferred_element_type=F32
    )


def remote(src, dst, send, recv, to):
    return pltpu.make_async_remote_copy(
        src_ref=src, dst_ref=dst, send_sem=send, recv_sem=recv, device_id=to, device_id_type=MESH
    )


def loop(low, high, step):
    def body(i, carry):
        step(i)
        return carry

    lax.fori_loop(low, high, body, 0)


def layer_kernel(
    nf_in, ng_in, small_in, giant_in, pn_in, pe_in, sc_in, win_in, bin_in, wout_in,
    nodes_out, small_out, giant_out, w_out, bias_out,
    nf, ng, win, wout, b_in, pn, pe, sc,
    etab, one_t, ix1, ixt, ix2, colb, rowb,
    esend, erecv, tsend, trecv, nd_all, og_all, pg_all, nt, nodes, smalls, giants,
    gw, gb, S, r0, S1, r1, S2, r2, G, bb0, bb1, bb2, bfin, gsend, grecv,
    in_sem, out_sem, gi_s, gi_r, i1_s, i1_r, i2_s, i2_r, e_s, e_r, t_s, t_r,
    w_s, w_r, b_s, b_r, gg_s, gg_r,
):
    g, u = lax.axis_index("grp"), lax.axis_index("sub")
    me = g * SUB + u
    y, zl, core, x, zh = g >> 2, (g >> 1) & 1, g & 1, u >> 1, u & 1
    z = zh * 2 + zl
    par = zl ^ (x & 1) ^ (y & 1)
    pm = (core << 6) | (par << 5) | (y << 3) | (x << 1) | zh
    there = (x, y, z)
    axis1 = (x, y, z)
    index2 = (y * 4 + z, z * 4 + x, x * 4 + y)

    def peer1(p, k):
        c = list(there)
        c[p] = k
        return device_of(c[0], c[1], c[2], core)

    def peer2(p, k):
        c = list(there)
        c[(p + 1) % 3] = k >> 2
        c[(p + 2) % 3] = k & 3
        return device_of(c[0], c[1], c[2], core)

    mine = pl.ds(pl.multiple_of(SMALL + u * GIANT, GIANT), GIANT)
    loads = [
        pltpu.make_async_copy(a, b, in_sem.at[i])
        for i, (a, b) in enumerate(
            (
                (pn_in, pn), (sc_in, sc), (giant_in, etab.at[mine]), (pe_in, pe),
                (small_in, etab.at[pl.ds(0, SMALL)]), (nf_in, nf), (ng_in, ng),
                (win_in, win), (wout_in, wout), (bin_in, b_in),
            )
        )
    ]
    for load in loads:
        load.start()

    barrier = pltpu.get_barrier_semaphore()
    loop(1, SUB, lambda o: pl.semaphore_signal(
        barrier, inc=1, device_id=(g, u ^ o), device_id_type=MESH))
    loop(1, GRP, lambda o: pl.semaphore_signal(
        barrier, inc=1, device_id=(g ^ o, u), device_id_type=MESH))

    loads[0].wait()
    loads[1].wait()
    r_at = lax.broadcasted_iota(I32, (8, 128), 0)
    l_at = lax.broadcasted_iota(I32, (8, 128), 1)
    spread = jnp.where((l_at >> 4) == r_at, sc[...].astype(F32), 0.0).astype(BF)
    j_at = lax.broadcasted_iota(I32, (128, 128), 0)
    p_at = lax.broadcasted_iota(I32, (128, 128), 1)
    expand = jnp.where((j_at & 15) == (p_at >> 3), 1.0, 0.0).astype(BF)
    counts = dot(spread, expand).astype(I32)
    packed = jnp.where((l_at & 7) < counts, pn[...] & (NODES - 1), 4095)
    ix1[u] = packed
    loads[2].wait()

    bb0[core] = jnp.zeros((8, 128), F32)

    pl.semaphore_wait(barrier, SUB + GRP - 2)

    def step1(o):
        to = (g, u ^ o)
        remote(ix1.at[u], ix1.at[u], i1_s, i1_r, to).start()
        remote(etab.at[mine], etab.at[mine], gi_s, gi_r, to).start()

    loop(1, SUB, step1)
    loads[3].wait()
    one_t[...] = jnp.where(
        lax.broadcasted_iota(I32, (EDGES, SLOTS), 0) == pe[...], 1.0, 0.0
    ).astype(BF)
    loads[4].wait()

    others = remote(ix1.at[pl.ds(0, SUB - 1)], ix1.at[pl.ds(0, SUB - 1)], i1_s, i1_r, (g, u ^ 1))
    others.wait_recv()

    for r in range(8):
        ixt[r] = jnp.concatenate([ix1[k, r : r + 1, :] for k in range(SUB)], axis=0)

    def step2(o):
        h = g ^ o
        remote(ixt.at[h >> 1], ix2.at[g], i2_s, i2_r, (h, u)).start()

    loop(1, GRP, step2)
    ix2[g] = ixt[g >> 1]

    span = pl.ds(SMALL, (SUB - 1) * GIANT)
    rows_in = remote(etab.at[span], etab.at[span], gi_s, gi_r, (g, u ^ 1))
    rows_in.wait_recv()
    esend[...] = dot(one_t[...], etab[...], 0, 0).astype(BF).reshape(DEVICES, CAP, WIDTH)

    def send_rows(s):
        j = me ^ mask_of(s)
        remote(esend.at[j], erecv.at[pm], e_s, e_r.at[s >> 5], place(j)).start()

    loop(1, DEVICES, send_rows)
    erecv[pm] = esend[me]

    half = ix2.at[pl.ds(0, GRP - 1)]
    terms_in = remote(half, half, i2_s, i2_r, (g ^ 1, u))
    terms_in.wait_recv()
    table = ix2[...].reshape(DEVICES, 128)
    high, low = (table >> 8).astype(F32).astype(BF), (table & 255).astype(F32).astype(BF)

    def source(q):
        qy, qx = (q >> 3) & 3, (q >> 1) & 3
        qz = ((q >> 5) & 1) ^ (qx & 1) ^ (qy & 1)
        return (qy << 5) | (qz << 4) | (((q >> 6) & 1) << 3) | (qx << 1) | (q & 1)

    first = (me & 15) * CAP
    s_col = lax.broadcasted_iota(I32, (SLOTS, 128), 0)
    d_col = lax.broadcasted_iota(I32, (SLOTS, 128), 1)
    pick = jnp.where(source(s_col >> 3) == d_col, 1.0, 0.0).astype(BF)
    values = dot(pick, high) * 256.0 + dot(pick, low)
    values = jnp.where(d_col == first + (s_col & 7), values, 0.0)
    col = jnp.sum(values, axis=1, keepdims=True).astype(I32)
    colb[...] = jnp.broadcast_to(col, (SLOTS, 128))
    values = dot(high, pick, 0, 1) * 256.0 + dot(low, pick, 0, 1)
    l_row = lax.broadcasted_iota(I32, (128, SLOTS), 0)
    s_row = lax.broadcasted_iota(I32, (128, SLOTS), 1)
    values = jnp.where(l_row == first + (s_row & 7), values, 0.0)
    rowb[...] = jnp.sum(values, axis=0, keepdims=True).astype(I32)

    for load in loads[5:]:
        load.wait()
    gw[...] = jnp.zeros_like(gw)
    gb[...] = jnp.zeros_like(gb)

    def chunk(c, last=False):
        b = (pm >> 5) ^ c
        rows = pl.ds(pl.multiple_of(b * ROWS, ROWS), ROWS)
        blocks = pl.ds(pl.multiple_of(b * PER, PER), PER)
        at = colb[rows]
        lanes = lax.broadcasted_iota(I32, (ROWS, 128), 1)
        hot = jnp.concatenate(
            [jnp.where(at == lanes + k * 128, 1.0, 0.0).astype(BF) for k in range(NODES // 128)],
            axis=1,
        )
        nd = dot(hot, nf[...]).astype(BF)
        og = dot(hot, ng[...]).astype(BF)
        nd_all[rows] = nd
        og_all[rows] = og
        preact = dot(nd, win[pl.ds(0, WIDTH)]) + b_in[...]
        hid_grad = dot(og, wout[...], 1, 1)

        if last:
            w = erecv.at[pl.ds(0, PER)]
            remote(w, w, e_s, e_r.at[c], (g, u ^ 1)).wait_recv()
        else:

            @pl.when(c == 0)
            def _():
                w = erecv.at[pl.ds(0, PER - 1)]
                remote(w, w, e_s, e_r.at[0], (g, u ^ 1)).wait_recv()

            @pl.when(c > 0)
            def _():
                w = erecv.at[pl.ds(0, PER)]
                remote(w, w, e_s, e_r.at[c], (g, u ^ 1)).wait_recv()

        er = erecv[blocks].reshape(ROWS, WIDTH)
        preact = preact + dot(er, win[pl.ds(WIDTH, WIDTH)])
        logistic = jax.nn.sigmoid(preact)
        hidden = (preact * logistic).astype(BF)
        pg = (hid_grad * logistic * (1.0 + preact * (1.0 - logistic))).astype(BF)
        pg_all[rows] = pg

        def weights(k, left, right):
            gw[pl.ds(k * WIDTH, WIDTH)] += dot(left, right, 0, 0)
            if last:
                reduce0(k)

        def terms():
            term = dot(pg, win[pl.ds(WIDTH, WIDTH)], 1, 1).astype(BF)
            tsend[blocks] = term.reshape(PER, CAP, WIDTH)

        if not last:
            terms()
            send_terms(c)
        weights(0, nd, pg)
        weights(1, er, pg)
        weights(2, hidden, og)
        gb[...] += jnp.sum(pg.astype(F32), axis=0, keepdims=True)
        if last:
            terms()

    def send_terms(c):
        def one(s):
            j = me ^ mask_of(s)
            remote(tsend.at[pm ^ s], trecv.at[me], t_s, t_r, place(j)).start()

        loop(c * PER + jnp.where(c == 0, 1, 0), (c + 1) * PER, one)

    twin = (g ^ 1, u)

    def reduce0(p):
        for h in range(2):
            for i in range(4):
                top, left = WIDTH * p + 256 * (i >> 1), 256 * h + 128 * (i & 1)
                S[h, p, i] = gw[top : top + 256, left : left + 128].astype(BF)
        remote(S.at[1 - core, p], r0.at[p], w_s.at[0, p], w_r.at[0, p], twin).start()

    loop(0, CHUNKS - 1, chunk)
    chunk(CHUNKS - 1, True)
    trecv[me] = tsend[pm]
    for i in range(4):
        bb0[core, i : i + 1, :] = gb[:, 128 * i : 128 * i + 128]
    bias0 = remote(bb0.at[core], bb0.at[core], b_s.at[0], b_r.at[0], twin)
    bias0.start()

    nt[...] = dot(pg_all[...], win[pl.ds(0, WIDTH)], 1, 1).astype(BF)

    def node_tile(t):
        rows = pl.ds(pl.multiple_of(t * 256, 256), 256)
        hot = jnp.where(
            lax.broadcasted_iota(I32, (256, SLOTS), 0) + t * 256 == rowb[...], 1.0, 0.0
        ).astype(BF)
        nodes[rows] = (ng[rows].astype(F32) + dot(hot, nt[...])).astype(BF)

    def settle(ref, stage, p):
        done = remote(ref, ref, w_s.at[stage, p], w_r.at[stage, p], twin)
        done.wait_recv()
        waits.append(done)

    waits = [bias0]
    loop(0, 2, node_tile)
    for p in range(3):
        settle(r0.at[p], 0, p)
        for i in range(4):
            rows, half = pl.ds(WIDTH * p + 256 * (i >> 1), 256), pl.ds(pl.multiple_of(256 * core + 128 * (i & 1), 128), 128)
            S1[p, i] = (gw[rows, half] + r0[p, i].astype(F32)).astype(BF)
        for o in range(1, 4):
            k = axis1[p] ^ o
            remote(S1.at[p, k], r1.at[p, axis1[p]], w_s.at[1, p], w_r.at[1, p], peer1(p, k)).start()
        r1[p, axis1[p]] = S1[p, axis1[p]]
    bias0.wait_recv()
    bb1[x] = bb0[0] + bb0[1]
    for o in range(1, 4):
        remote(bb1.at[x], bb1.at[x], b_s.at[1], b_r.at[1], peer1(0, x ^ o)).start()
    send_terms(CHUNKS - 1)

    loop(2, NODES // 256, node_tile)
    put_nodes = pltpu.make_async_copy(nodes, nodes_out, out_sem.at[0])
    put_nodes.start()

    for p in range(3):
        settle(r1.at[p, pl.ds(0, 3)], 1, p)
        total = r1[p, 0].astype(F32) + r1[p, 1].astype(F32) + r1[p, 2].astype(F32) + r1[p, 3].astype(F32)
        S2[p] = total.astype(BF).reshape(16, 16, 128)

        def give2(o, p=p):
            k = index2[p] ^ o
            remote(S2.at[p, k], r2.at[p, index2[p]], w_s.at[2, p], w_r.at[2, p], peer2(p, k)).start()

        loop(1, 16, give2)
        r2[p, index2[p]] = S2[p, index2[p]]
    half_b1 = bb1.at[pl.ds(0, 3)]
    wait_b1 = remote(half_b1, half_b1, b_s.at[1], b_r.at[1], twin)
    wait_b1.wait_recv()
    bb2[index2[0]] = bb1[0] + bb1[1] + bb1[2] + bb1[3]

    def give_bias(o):
        remote(bb2.at[index2[0]], bb2.at[index2[0]], b_s.at[2], b_r.at[2], peer2(0, index2[0] ^ o)).start()

    loop(1, 16, give_bias)

    back = trecv.at[pl.ds(0, DEVICES - 1)]
    wait_t = remote(back, back, t_s, t_r, twin)
    wait_t.wait_recv()
    edge_sum = dot(one_t[...], trecv[...].reshape(SLOTS, WIDTH))
    gsend[...] = edge_sum[SMALL:].astype(BF).reshape(SUB, GIANT, WIDTH)

    def give_giants(o):
        remote(gsend.at[u ^ o], grecv.at[u], gg_s, gg_r, (g, u ^ o)).start()

    loop(1, SUB, give_giants)
    grecv[u] = gsend[u]
    smalls[...] = edge_sum[:SMALL].astype(BF)
    put_small = pltpu.make_async_copy(smalls, small_out, out_sem.at[1])
    put_small.start()

    for p in range(3):
        settle(r2.at[p, pl.ds(0, 15)], 2, p)
        G[core, p, axis1[p], index2[p]] = jnp.sum(r2[p].astype(F32), axis=0).astype(BF)

        def share2(o, p=p):
            piece = G.at[core, p, axis1[p], index2[p]]
            remote(piece, piece, w_s.at[3, p], w_r.at[3, p], peer2(p, index2[p] ^ o)).start()

        loop(1, 16, share2)

    for p in range(3):
        settle(r2.at[p, pl.ds(0, 15)], 3, p)
        for o in range(1, 4):
            piece = G.at[core, p, axis1[p]]
            remote(piece, piece, w_s.at[4, p], w_r.at[4, p], peer1(p, axis1[p] ^ o)).start()

    half_g = grecv.at[pl.ds(0, SUB - 1)]
    wait_g = remote(half_g, half_g, gg_s, gg_r, twin)
    wait_g.wait_recv()
    giants[...] = jnp.sum(grecv[...].astype(F32), axis=0).astype(BF)
    put_giant = pltpu.make_async_copy(giants, giant_out, out_sem.at[2])
    put_giant.start()

    half_b2 = bb2.at[pl.ds(0, 15)]
    wait_b2 = remote(half_b2, half_b2, b_s.at[2], b_r.at[2], twin)
    wait_b2.wait_recv()
    bias = jnp.sum(bb2[...], axis=0)
    for i in range(4):
        bfin[:, 128 * i : 128 * i + 128] = bias[i : i + 1]
    put_bias = pltpu.make_async_copy(bfin, bias_out, out_sem.at[3])
    put_bias.start()

    puts = [put_nodes, put_small, put_giant, put_bias]
    for p in range(3):
        settle(r1.at[p, pl.ds(0, 3)], 4, p)
        remote(G.at[core, p], G.at[core, p], w_s.at[5, p], w_r.at[5, p], twin).start()
        puts.append(pltpu.make_async_copy(G.at[core, p], w_out.at[core, p], out_sem.at[4 + p]))
        puts[-1].start()
    for p in range(3):
        settle(r0.at[p], 5, p)
        puts.append(pltpu.make_async_copy(G.at[1 - core, p], w_out.at[1 - core, p], out_sem.at[7 + p]))
        puts[-1].start()

    others.wait_send()
    rows_in.wait_send()
    terms_in.wait_send()
    sent = esend.at[pl.ds(0, DEVICES - 1)]
    remote(sent, sent, e_s, e_r.at[0], twin).wait_send()
    for one in (wait_t, wait_b1, wait_b2, wait_g, *waits):
        one.wait_send()
    for one in puts:
        one.wait()


def layer(node_feats, node_grad, small_edges, giant_edges, pair_node, pair_edge, send_count, w_in, b_in, w_out):
    V = pltpu.VMEM
    dma = pltpu.SemaphoreType.DMA
    any_spec = pl.BlockSpec(memory_space=pl.ANY)
    wide = (DEVICES, CAP, WIDTH)
    shape = jax.ShapeDtypeStruct
    return pl.pallas_call(
        layer_kernel,
        out_shape=(
            shape((NODES, WIDTH), BF),
            shape((SMALL, WIDTH), BF),
            shape((GIANT, WIDTH), BF),
            shape((2, 3, 4, 16, 16, 128), BF),
            shape((1, WIDTH), F32),
        ),
        in_specs=[any_spec] * 10,
        out_specs=(any_spec,) * 5,
        scratch_shapes=[
            V((NODES, WIDTH), BF), V((NODES, WIDTH), BF), V((2 * WIDTH, WIDTH), BF), V((WIDTH, WIDTH), BF),
            V((1, WIDTH), F32), V((8, 128), I32), V((1, SLOTS), I32), V((1, 128), I32),
            V((EDGES, WIDTH), BF), V((EDGES, SLOTS), BF), V((SUB, 8, 128), I32), V((8, SUB, 128), I32), V((GRP, SUB, 128), I32),
            V((SLOTS, 128), I32), V((1, SLOTS), I32),
            V(wide, BF), V(wide, BF), V(wide, BF), V(wide, BF),
            V((SLOTS, WIDTH), BF), V((SLOTS, WIDTH), BF), V((SLOTS, WIDTH), BF), V((SLOTS, WIDTH), BF),
            V((NODES, WIDTH), BF), V((SMALL, WIDTH), BF), V((GIANT, WIDTH), BF),
            V((3 * WIDTH, WIDTH), F32), V((1, WIDTH), F32),
            V((2, 3, 4, 256, 128), BF), V((3, 4, 256, 128), BF),
            V((3, 4, 256, 128), BF), V((3, 4, 256, 128), BF),
            V((3, 16, 16, 128), BF), V((3, 16, 16, 128), BF), V((2, 3, 4, 16, 16, 128), BF),
            V((2, 8, 128), F32), V((4, 8, 128), F32), V((16, 8, 128), F32), V((1, WIDTH), F32),
            V((SUB, GIANT, WIDTH), BF), V((SUB, GIANT, WIDTH), BF),
            dma((10,)), dma((10,)), dma, dma, dma, dma, dma, dma, dma, dma((CHUNKS,)), dma, dma,
            dma((6, 3)), dma((6, 3)), dma((3,)), dma((3,)), dma, dma,
        ],
        compiler_params=pltpu.CompilerParams(
            collective_id=1, has_side_effects=True, vmem_limit_bytes=56 << 20
        ),
        name="layer",
    )(node_feats, node_grad, small_edges, giant_edges, pair_node, pair_edge, send_count, w_in, b_in, w_out)


def finish_kernel(
    nodes_in, small_in, giant_in, w_in, bias_in,
    nodes_out, small_out, giant_out, gi_out, gb_out, go_out,
    nodes, small, giant, bias, parts, wide, in_sem, out_sem,
):
    through = (
        (nodes_in, nodes, nodes_out), (small_in, small, small_out), (giant_in, giant, giant_out), (bias_in, bias, gb_out),
    )
    loads = [pltpu.make_async_copy(w_in.at[:, p], parts.at[:, p], in_sem.at[p]) for p in range(3)]
    loads += [pltpu.make_async_copy(a, b, in_sem.at[3 + i]) for i, (a, b, _) in enumerate(through)]
    for one in loads:
        one.start()
    puts = []
    for p in range(3):
        loads[p].wait()
        for h in range(2):
            for i in range(4):
                top, left = 256 * (i >> 1), 256 * h + 128 * (i & 1)
                wide[p, top : top + 256, left : left + 128] = parts[h, p, i].reshape(256, 128).astype(F32)
        out = gi_out.at[pl.ds(WIDTH * p, WIDTH)] if p < 2 else go_out
        puts.append(pltpu.make_async_copy(wide.at[p], out, out_sem.at[p]))
        puts[-1].start()
    for i, (_, a, b) in enumerate(through):
        loads[3 + i].wait()
        puts.append(pltpu.make_async_copy(a, b, out_sem.at[3 + i]))
        puts[-1].start()
    for one in puts:
        one.wait()


def finish(*arrays):
    any_spec = pl.BlockSpec(memory_space=pl.ANY)
    shape = jax.ShapeDtypeStruct
    return pl.pallas_call(
        finish_kernel,
        out_shape=(
            shape((NODES, WIDTH), BF), shape((SMALL, WIDTH), BF), shape((GIANT, WIDTH), BF),
            shape((2 * WIDTH, WIDTH), F32), shape((1, WIDTH), F32), shape((WIDTH, WIDTH), F32),
        ),
        in_specs=[any_spec] * 5,
        out_specs=(any_spec,) * 6,
        scratch_shapes=[
            pltpu.VMEM((NODES, WIDTH), BF), pltpu.VMEM((SMALL, WIDTH), BF), pltpu.VMEM((GIANT, WIDTH), BF),
            pltpu.VMEM((1, WIDTH), F32), pltpu.VMEM((2, 3, 4, 16, 16, 128), BF), pltpu.VMEM((3, WIDTH, WIDTH), F32),
            pltpu.SemaphoreType.DMA((7,)), pltpu.SemaphoreType.DMA((7,)),
        ],
        compiler_params=pltpu.CompilerParams(vmem_limit_bytes=60 << 20),
        name="finish",
    )(*arrays)


def shards(
    node_feats, node_grad, small_edges, giant_edges, pair_node, pair_edge, send_count, w_in, b_in, w_out
):
    out = finish(*layer(
        node_feats, node_grad, small_edges, giant_edges, pair_node.reshape(8, 128),
        pair_edge.reshape(1, SLOTS), send_count, w_in, b_in.reshape(1, WIDTH), w_out,
    ))
    return (*out[:4], out[4].reshape(WIDTH), out[5])


def solution(mesh):
    both = ("grp", "sub")
    placed = (
        P(both, None), P(both, None), P(both, None), P(both, None), P(both), P(both), P(both, None), P(), P(), P(),
    )
    return jax.shard_map(
        shards,
        mesh=mesh,
        in_specs=placed,
        out_specs=(P(both, None), P(both, None), P(both, None), P(), P(), P()),
        check_vma=False,
    )
```

time: 383 us -> 69.4 us (0.18)
  waiting for transfers between devices: 147 us -> 0 us
  blocking collectives: 110 us -> 0 us
  Pallas kernels: 0 us -> 68.6 us
  other arithmetic: 39.1 us -> 0 us
  local copies, waits for them, and re-layouts: 31.8 us -> 0 us
  starting transfers between devices: 28.2 us -> 0 us
  between operations: 14.3 us -> 0.64 us
  matrix products: 12.3 us -> 0 us
    psum x2 -> x0, waiting for transfers between devices: 142 us -> none  [the longest x1 142 us: shards(): lax.psum((grad_in, grad_bias, grad_out), ('grp', 'sub'))]
    pallas_call x0 -> x2, Pallas kernels: none -> 68.6 us  [the longest x1 64.9 us: layer(): pl.pallas_call(layer_kernel, out_shape=(shape((NODES, WIDTH), BF), shape(...]
    psum x1 -> x0, blocking collectives: 68.5 us -> none  [shards(): lax.psum((grad_in, grad_bias, grad_out), ('grp', 'sub'))]
    all_gather x1 -> x0, blocking collectives: 41.6 us -> none  [shards(): giant_group = lax.all_gather(giant_edges, 'sub', axis=0, tiled=True)]
    all_to_all x3 -> x0, starting transfers between devices: 28.2 us -> none  [the longest x1 12 us: move_terms(): lax.all_to_all(values, ('grp', 'sub'), split_axis=0, concat_axis=0, tiled...]
    gather x3 -> x0, local copies, waits for them, and re-layouts: 19.4 us -> none  [the longest x1 7.7 us: shards(): jnp.take(owner_table, requested, axis=0)]
    scatter-add x2 -> x0, other arithmetic: 18.9 us -> none  [the longest x1 11.3 us: shards(): jax.ops.segment_sum(returned.astype(jnp.float32), requested, num_segments...]
    dot_general x5 -> x0, matrix products: 12.3 us -> none  [the longest x1 4.14 us: shards(): jnp.einsum('pk,ph->kh', joined, pre_grad, preferred_element_type=jnp.floa...]
  transfers between devices with their start and end apart: 5 -> 0, of which waited for: 2 -> 0; matrix products, arithmetic and copies ran while one was open for 13% -> 0% of each run, Pallas kernels for 0% -> 0%
where the time goes in v2:
time: 69.4 us; the launch traced here: 69.2 us
  Pallas kernels  68.6 us (99%)
    pallas_call x1, Pallas kernels, layer(): pl.pallas_call(layer_kernel, out_shape=(shape((NODES, WIDTH), BF), shape(...  64.9 us
    pallas_call x1, Pallas kernels, finish(): pl.pallas_call(finish_kernel, out_shape=(shape((NODES, WIDTH), BF), shape...  3.72 us

profile of v2, /device:TPU:1, one launch (start us, length us, event | category | flops | bytes accessed | tf_op | source)
XLA Modules:
  0.0 69.2 jit_solution(12283478254288656203)
XLA Ops:
  0.6 64.9 %layer.1 = (bf16[2048,512]{1,0:T(8,128)(2,1)}, bf16[256,512]{1,0:T(8,128)(2,1)}, bf16[16,512]{1,0:T(8,128)(2,1)}, bf16[2,3,4,16,16,128]{5,4,3,2,1,0:T(8,128)(2,1)}, f32[1,512]{1,0:T(1,128)}) custom-call(bf16[2048,512]{1,0:T(8,128)(2,1)} %nf_in.1, bf16[2048,512]{1,0:T(8,128)(2,1)} %ng_in.1, bf16[256,512]{1,0:T(8,128)(2,1)} %small_in.1, ...), custom_call_target="tpu_custom_call" | custom-call | tf_op jit(solution)/shard_map/layer/pallas_call | solution.py:411
  65.5 3.7 %finish.1 = (bf16[2048,512]{1,0:T(8,128)(2,1)}, bf16[256,512]{1,0:T(8,128)(2,1)}, bf16[16,512]{1,0:T(8,128)(2,1)}, f32[1024,512]{1,0:T(8,128)}, f32[1,512]{1,0:T(1,128)}, /*index=5*/f32[512,512]{1,0:T(8,128)}) custom-call(bf16[2048,512]{1,0:T(8,128)(2,1)} %get-tuple-element.17.nodes_in, bf16[256,512]{1,0:T(8,128)(2,1)} %get-tuple-element.18.small_in, ...), custom_call_target="tpu_custom_call" | custom-call | tf_op jit(solution)/shard_map/finish/pallas_call | solution.py:479

commit v3 on v2

--- a/solution.py
+++ b/solution.py
@@ -1,5 +1,3 @@
-import functools
-
 import jax
 import jax.numpy as jnp
 from jax import lax
@@ -22,6 +20,7 @@
 GIANT = 16
 EDGES = SMALL + GIANT * SUB
 CHUNKS = 4
+FAR = (10, 9, 11, 6, 14, 2, 8, 5, 7, 13, 15, 1, 3, 4, 12)
 PER = DEVICES // CHUNKS
 ROWS = PER * CAP
 
@@ -62,12 +61,12 @@
 
 def layer_kernel(
     nf_in, ng_in, small_in, giant_in, pn_in, pe_in, sc_in, win_in, bin_in, wout_in,
-    nodes_out, small_out, giant_out, w_out, bias_out,
+    nodes, smalls, giants, wide, bfin,
     nf, ng, win, wout, b_in, pn, pe, sc,
     etab, one_t, ix1, ixt, ix2, colb, rowb,
-    esend, erecv, tsend, trecv, nd_all, og_all, pg_all, nt, nodes, smalls, giants,
-    gw, gb, S, r0, S1, r1, S2, r2, G, bb0, bb1, bb2, bfin, gsend, grecv,
-    in_sem, out_sem, gi_s, gi_r, i1_s, i1_r, i2_s, i2_r, e_s, e_r, t_s, t_r,
+    esend, erecv, tsend, trecv, nd_all, og_all, pg_all, nt,
+    gw, gb, S, r0, S1, r1, S2, r2, G, bb0, bb1, bb2, gsend, grecv,
+    in_sem, gi_s, gi_r, i1_s, i1_r, i2_s, i2_r, e_s, e_r, t_s, t_r,
     w_s, w_r, b_s, b_r, gg_s, gg_r,
 ):
     g, u = lax.axis_index("grp"), lax.axis_index("sub")
@@ -128,12 +127,10 @@
 
     pl.semaphore_wait(barrier, SUB + GRP - 2)
 
-    def step1(o):
-        to = (g, u ^ o)
-        remote(ix1.at[u], ix1.at[u], i1_s, i1_r, to).start()
-        remote(etab.at[mine], etab.at[mine], gi_s, gi_r, to).start()
-
-    loop(1, SUB, step1)
+    for o in (5, 4, 7, 3, 6, 2, 1):
+        remote(etab.at[mine], etab.at[mine], gi_s, gi_r, (g, u ^ o)).start()
+    for o in (5, 4, 7, 3, 6, 2, 1):
+        remote(ix1.at[u], ix1.at[u], i1_s, i1_r, (g, u ^ o)).start()
     loads[3].wait()
     one_t[...] = jnp.where(
         lax.broadcasted_iota(I32, (EDGES, SLOTS), 0) == pe[...], 1.0, 0.0
@@ -255,8 +252,7 @@
 
     def send_terms(c):
         def one(s):
-            j = me ^ mask_of(s)
-            remote(tsend.at[pm ^ s], trecv.at[me], t_s, t_r, place(j)).start()
+            remote(tsend.at[pm ^ s], trecv.at[me], t_s, t_r, place(me ^ mask_of(s))).start()
 
         loop(c * PER + jnp.where(c == 0, 1, 0), (c + 1) * PER, one)
 
@@ -292,25 +288,23 @@
         waits.append(done)
 
     waits = [bias0]
+    send_terms(CHUNKS - 1)
     loop(0, 2, node_tile)
     for p in range(3):
         settle(r0.at[p], 0, p)
         for i in range(4):
             rows, half = pl.ds(WIDTH * p + 256 * (i >> 1), 256), pl.ds(pl.multiple_of(256 * core + 128 * (i & 1), 128), 128)
             S1[p, i] = (gw[rows, half] + r0[p, i].astype(F32)).astype(BF)
-        for o in range(1, 4):
+        for o in (2, 1, 3):
             k = axis1[p] ^ o
             remote(S1.at[p, k], r1.at[p, axis1[p]], w_s.at[1, p], w_r.at[1, p], peer1(p, k)).start()
         r1[p, axis1[p]] = S1[p, axis1[p]]
     bias0.wait_recv()
     bb1[x] = bb0[0] + bb0[1]
-    for o in range(1, 4):
+    for o in (2, 1, 3):
         remote(bb1.at[x], bb1.at[x], b_s.at[1], b_r.at[1], peer1(0, x ^ o)).start()
-    send_terms(CHUNKS - 1)
 
     loop(2, NODES // 256, node_tile)
-    put_nodes = pltpu.make_async_copy(nodes, nodes_out, out_sem.at[0])
-    put_nodes.start()
 
     for p in range(3):
         settle(r1.at[p, pl.ds(0, 3)], 1, p)
@@ -321,7 +315,8 @@
             k = index2[p] ^ o
             remote(S2.at[p, k], r2.at[p, index2[p]], w_s.at[2, p], w_r.at[2, p], peer2(p, k)).start()
 
-        loop(1, 16, give2)
+        for o in FAR:
+            give2(o)
         r2[p, index2[p]] = S2[p, index2[p]]
     half_b1 = bb1.at[pl.ds(0, 3)]
     wait_b1 = remote(half_b1, half_b1, b_s.at[1], b_r.at[1], twin)
@@ -333,6 +328,18 @@
 
     loop(1, 16, give_bias)
 
+    for p in range(3):
+        settle(r2.at[p, pl.ds(0, 15)], 2, p)
+        G[core, p, axis1[p], index2[p]] = jnp.sum(r2[p].astype(F32), axis=0).astype(BF)
+
+        def share2(o, p=p):
+            piece = G.at[core, p, axis1[p], index2[p]]
+            remote(piece, piece, w_s.at[3, p], w_r.at[3, p], peer2(p, index2[p] ^ o)).start()
+
+        for o in FAR:
+            share2(o)
+
+
     back = trecv.at[pl.ds(0, DEVICES - 1)]
     wait_t = remote(back, back, t_s, t_r, twin)
     wait_t.wait_recv()
@@ -345,22 +352,10 @@
     loop(1, SUB, give_giants)
     grecv[u] = gsend[u]
     smalls[...] = edge_sum[:SMALL].astype(BF)
-    put_small = pltpu.make_async_copy(smalls, small_out, out_sem.at[1])
-    put_small.start()
-
-    for p in range(3):
-        settle(r2.at[p, pl.ds(0, 15)], 2, p)
-        G[core, p, axis1[p], index2[p]] = jnp.sum(r2[p].astype(F32), axis=0).astype(BF)
-
-        def share2(o, p=p):
-            piece = G.at[core, p, axis1[p], index2[p]]
-            remote(piece, piece, w_s.at[3, p], w_r.at[3, p], peer2(p, index2[p] ^ o)).start()
-
-        loop(1, 16, share2)
 
     for p in range(3):
         settle(r2.at[p, pl.ds(0, 15)], 3, p)
-        for o in range(1, 4):
+        for o in (2, 1, 3):
             piece = G.at[core, p, axis1[p]]
             remote(piece, piece, w_s.at[4, p], w_r.at[4, p], peer1(p, axis1[p] ^ o)).start()
 
@@ -368,8 +363,6 @@
     wait_g = remote(half_g, half_g, gg_s, gg_r, twin)
     wait_g.wait_recv()
     giants[...] = jnp.sum(grecv[...].astype(F32), axis=0).astype(BF)
-    put_giant = pltpu.make_async_copy(giants, giant_out, out_sem.at[2])
-    put_giant.start()
 
     half_b2 = bb2.at[pl.ds(0, 15)]
     wait_b2 = remote(half_b2, half_b2, b_s.at[2], b_r.at[2], twin)
@@ -377,19 +370,21 @@
     bias = jnp.sum(bb2[...], axis=0)
     for i in range(4):
         bfin[:, 128 * i : 128 * i + 128] = bias[i : i + 1]
-    put_bias = pltpu.make_async_copy(bfin, bias_out, out_sem.at[3])
-    put_bias.start()
-
-    puts = [put_nodes, put_small, put_giant, put_bias]
+
+
+    def widen(h, p):
+        for i in range(4):
+            top, left = 256 * (i >> 1), pl.multiple_of(256 * h + 128 * (i & 1), 128)
+            wide[p, top : top + 256, pl.ds(left, 128)] = G[h, p, i].reshape(256, 128).astype(F32)
+
     for p in range(3):
         settle(r1.at[p, pl.ds(0, 3)], 4, p)
         remote(G.at[core, p], G.at[core, p], w_s.at[5, p], w_r.at[5, p], twin).start()
-        puts.append(pltpu.make_async_copy(G.at[core, p], w_out.at[core, p], out_sem.at[4 + p]))
-        puts[-1].start()
+    for p in range(3):
+        widen(core, p)
     for p in range(3):
         settle(r0.at[p], 5, p)
-        puts.append(pltpu.make_async_copy(G.at[1 - core, p], w_out.at[1 - core, p], out_sem.at[7 + p]))
-        puts[-1].start()
+        widen(1 - core, p)
 
     others.wait_send()
     rows_in.wait_send()
@@ -398,27 +393,24 @@
     remote(sent, sent, e_s, e_r.at[0], twin).wait_send()
     for one in (wait_t, wait_b1, wait_b2, wait_g, *waits):
         one.wait_send()
-    for one in puts:
-        one.wait()
-
-
-def layer(node_feats, node_grad, small_edges, giant_edges, pair_node, pair_edge, send_count, w_in, b_in, w_out):
+
+
+def layer(*arrays):
     V = pltpu.VMEM
     dma = pltpu.SemaphoreType.DMA
     any_spec = pl.BlockSpec(memory_space=pl.ANY)
     wide = (DEVICES, CAP, WIDTH)
-    shape = jax.ShapeDtypeStruct
     return pl.pallas_call(
         layer_kernel,
         out_shape=(
-            shape((NODES, WIDTH), BF),
-            shape((SMALL, WIDTH), BF),
-            shape((GIANT, WIDTH), BF),
-            shape((2, 3, 4, 16, 16, 128), BF),
-            shape((1, WIDTH), F32),
+            V((NODES, WIDTH), BF),
+            V((SMALL, WIDTH), BF),
+            V((GIANT, WIDTH), BF),
+            V((3, WIDTH, WIDTH), F32),
+            V((1, WIDTH), F32),
         ),
         in_specs=[any_spec] * 10,
-        out_specs=(any_spec,) * 5,
+        out_specs=(pl.BlockSpec(memory_space=V),) * 5,
         scratch_shapes=[
             V((NODES, WIDTH), BF), V((NODES, WIDTH), BF), V((2 * WIDTH, WIDTH), BF), V((WIDTH, WIDTH), BF),
             V((1, WIDTH), F32), V((8, 128), I32), V((1, SLOTS), I32), V((1, 128), I32),
@@ -426,55 +418,34 @@
             V((SLOTS, 128), I32), V((1, SLOTS), I32),
             V(wide, BF), V(wide, BF), V(wide, BF), V(wide, BF),
             V((SLOTS, WIDTH), BF), V((SLOTS, WIDTH), BF), V((SLOTS, WIDTH), BF), V((SLOTS, WIDTH), BF),
-            V((NODES, WIDTH), BF), V((SMALL, WIDTH), BF), V((GIANT, WIDTH), BF),
             V((3 * WIDTH, WIDTH), F32), V((1, WIDTH), F32),
             V((2, 3, 4, 256, 128), BF), V((3, 4, 256, 128), BF),
             V((3, 4, 256, 128), BF), V((3, 4, 256, 128), BF),
             V((3, 16, 16, 128), BF), V((3, 16, 16, 128), BF), V((2, 3, 4, 16, 16, 128), BF),
-            V((2, 8, 128), F32), V((4, 8, 128), F32), V((16, 8, 128), F32), V((1, WIDTH), F32),
+            V((2, 8, 128), F32), V((4, 8, 128), F32), V((16, 8, 128), F32),
             V((SUB, GIANT, WIDTH), BF), V((SUB, GIANT, WIDTH), BF),
-            dma((10,)), dma((10,)), dma, dma, dma, dma, dma, dma, dma, dma((CHUNKS,)), dma, dma,
+            dma((10,)), dma, dma, dma, dma, dma, dma, dma, dma((CHUNKS,)), dma, dma,
             dma((6, 3)), dma((6, 3)), dma((3,)), dma((3,)), dma, dma,
         ],
         compiler_params=pltpu.CompilerParams(
-            collective_id=1, has_side_effects=True, vmem_limit_bytes=56 << 20
+            collective_id=1, has_side_effects=True, vmem_limit_bytes=48 << 20
         ),
         name="layer",
-    )(node_feats, node_grad, small_edges, giant_edges, pair_node, pair_edge, send_count, w_in, b_in, w_out)
-
-
-def finish_kernel(
-    nodes_in, small_in, giant_in, w_in, bias_in,
-    nodes_out, small_out, giant_out, gi_out, gb_out, go_out,
-    nodes, small, giant, bias, parts, wide, in_sem, out_sem,
-):
-    through = (
-        (nodes_in, nodes, nodes_out), (small_in, small, small_out), (giant_in, giant, giant_out), (bias_in, bias, gb_out),
-    )
-    loads = [pltpu.make_async_copy(w_in.at[:, p], parts.at[:, p], in_sem.at[p]) for p in range(3)]
-    loads += [pltpu.make_async_copy(a, b, in_sem.at[3 + i]) for i, (a, b, _) in enumerate(through)]
-    for one in loads:
+    )(*[pltpu.with_memory_space_constraint(a, pltpu.HBM) for a in arrays])
+
+
+def finish_kernel(nodes, small, giant, wide, bias, nodes_out, small_out, giant_out, gi_out, gb_out, go_out, sem):
+    pairs = [(wide.at[p], gi_out.at[pl.ds(WIDTH * p, WIDTH)]) for p in range(2)] + [(wide.at[2], go_out)]
+    pairs += [(nodes, nodes_out), (small, small_out), (giant, giant_out), (bias, gb_out)]
+    puts = [pltpu.make_async_copy(a, b, sem.at[i]) for i, (a, b) in enumerate(pairs)]
+    for one in puts:
         one.start()
-    puts = []
-    for p in range(3):
-        loads[p].wait()
-        for h in range(2):
-            for i in range(4):
-                top, left = 256 * (i >> 1), 256 * h + 128 * (i & 1)
-                wide[p, top : top + 256, left : left + 128] = parts[h, p, i].reshape(256, 128).astype(F32)
-        out = gi_out.at[pl.ds(WIDTH * p, WIDTH)] if p < 2 else go_out
-        puts.append(pltpu.make_async_copy(wide.at[p], out, out_sem.at[p]))
-        puts[-1].start()
-    for i, (_, a, b) in enumerate(through):
-        loads[3 + i].wait()
-        puts.append(pltpu.make_async_copy(a, b, out_sem.at[3 + i]))
-        puts[-1].start()
     for one in puts:
         one.wait()
 
 
 def finish(*arrays):
-    any_spec = pl.BlockSpec(memory_space=pl.ANY)
+    held = [pltpu.with_memory_space_constraint(a, pltpu.VMEM) for a in arrays]
     shape = jax.ShapeDtypeStruct
     return pl.pallas_call(
         finish_kernel,
@@ -482,16 +453,12 @@
             shape((NODES, WIDTH), BF), shape((SMALL, WIDTH), BF), shape((GIANT, WIDTH), BF),
             shape((2 * WIDTH, WIDTH), F32), shape((1, WIDTH), F32), shape((WIDTH, WIDTH), F32),
         ),
-        in_specs=[any_spec] * 5,
-        out_specs=(any_spec,) * 6,
-        scratch_shapes=[
-            pltpu.VMEM((NODES, WIDTH), BF), pltpu.VMEM((SMALL, WIDTH), BF), pltpu.VMEM((GIANT, WIDTH), BF),
-            pltpu.VMEM((1, WIDTH), F32), pltpu.VMEM((2, 3, 4, 16, 16, 128), BF), pltpu.VMEM((3, WIDTH, WIDTH), F32),
-            pltpu.SemaphoreType.DMA((7,)), pltpu.SemaphoreType.DMA((7,)),
-        ],
-        compiler_params=pltpu.CompilerParams(vmem_limit_bytes=60 << 20),
+        in_specs=[pl.BlockSpec(memory_space=pltpu.VMEM)] * 5,
+        out_specs=(pl.BlockSpec(memory_space=pl.ANY),) * 6,
+        scratch_shapes=[pltpu.SemaphoreType.DMA((7,))],
+        compiler_params=pltpu.CompilerParams(vmem_limit_bytes=16 << 20),
         name="finish",
-    )(*arrays)
+    )(*held)
 
 
 def shards(

time: 69.4 us -> 65.4 us (0.942)
  Pallas kernels: 68.6 us -> 64.6 us
    pallas_call x1, Pallas kernels: 64.9 us -> 62.1 us  [layer(): pl.pallas_call(layer_kernel, out_shape=(V((NODES, WIDTH), BF), V((SMALL,...]
    pallas_call x1, Pallas kernels: 3.72 us -> 2.5 us  [finish(): pl.pallas_call(finish_kernel, out_shape=(shape((NODES, WIDTH), BF), shape...]
where the time goes in v3:
time: 65.4 us; the launch traced here: 65.3 us
  Pallas kernels  64.6 us (99%)
    pallas_call x1, Pallas kernels, layer(): pl.pallas_call(layer_kernel, out_shape=(V((NODES, WIDTH), BF), V((SMALL,...  62.1 us
    pallas_call x1, Pallas kernels, finish(): pl.pallas_call(finish_kernel, out_shape=(shape((NODES, WIDTH), BF), shape...  2.5 us

profile of v3, /device:TPU:1, one launch (start us, length us, event | category | flops | bytes accessed | tf_op | source)
XLA Modules:
  0.0 65.3 jit_solution(2766215902089000254)
XLA Ops:
  0.6 62.1 %layer.1 = (bf16[2048,512]{1,0:T(8,128)(2,1)S(1)}, bf16[256,512]{1,0:T(8,128)(2,1)S(1)}, bf16[16,512]{1,0:T(8,128)(2,1)S(1)}, f32[3,512,512]{2,1,0:T(8,128)S(1)}, f32[1,512]{1,0:T(1,128)S(1)}) custom-call(bf16[2048,512]{1,0:T(8,128)(2,1)} %nf_in.1, bf16[2048,512]{1,0:T(8,128)(2,1)} %ng_in.1, bf16[256,512]{1,0:T(8,128)(2,1)} %small_in.1, ...), custom_call_target="tpu_custom_call" | custom-call | tf_op jit(solution)/shard_map/layer/pallas_call | solution.py:403
  62.8 2.5 %finish.1 = (bf16[2048,512]{1,0:T(8,128)(2,1)}, bf16[256,512]{1,0:T(8,128)(2,1)}, bf16[16,512]{1,0:T(8,128)(2,1)}, f32[1024,512]{1,0:T(8,128)}, f32[1,512]{1,0:T(1,128)}, /*index=5*/f32[512,512]{1,0:T(8,128)}) custom-call(bf16[2048,512]{1,0:T(8,128)(2,1)S(1)} %get-tuple-element.17.nodes, bf16[256,512]{1,0:T(8,128)(2,1)S(1)} %get-tuple-element.18.small, ...), custom_call_target="tpu_custom_call" | custom-call | tf_op jit(solution)/shard_map/finish/pallas_call | solution.py:450

commit v4 on v3

--- a/solution.py
+++ b/solution.py
@@ -19,7 +19,7 @@
 SMALL = 256
 GIANT = 16
 EDGES = SMALL + GIANT * SUB
-CHUNKS = 4
+CHUNKS = 8
 FAR = (10, 9, 11, 6, 14, 2, 8, 5, 7, 13, 15, 1, 3, 4, 12)
 PER = DEVICES // CHUNKS
 ROWS = PER * CAP
@@ -30,8 +30,9 @@
 
 
 def mask_of(s):
-    core, par, y, x, zh = (s >> 6) & 1, (s >> 5) & 1, (s >> 3) & 3, (s >> 1) & 3, s & 1
-    zl = par ^ (x & 1) ^ (y & 1)
+    core, y, x = (s >> 6) & 1, (s >> 2) & 3, s & 3
+    zl = ((s >> 5) & 1) ^ (x & 1) ^ (y & 1)
+    zh = ((s >> 4) & 1) ^ (x >> 1) ^ (y >> 1)
     return (y << 5) | (zl << 4) | (core << 3) | (x << 1) | zh
 
 
@@ -64,7 +65,7 @@
     nodes, smalls, giants, wide, bfin,
     nf, ng, win, wout, b_in, pn, pe, sc,
     etab, one_t, ix1, ixt, ix2, colb, rowb,
-    esend, erecv, tsend, trecv, nd_all, og_all, pg_all, nt,
+    esend, erecv, tsend, trecv, nd_all, og_all, pg_all, hid_all, nt, pre_n, hid_n,
     gw, gb, S, r0, S1, r1, S2, r2, G, bb0, bb1, bb2, gsend, grecv,
     in_sem, gi_s, gi_r, i1_s, i1_r, i2_s, i2_r, e_s, e_r, t_s, t_r,
     w_s, w_r, b_s, b_r, gg_s, gg_r,
@@ -73,8 +74,7 @@
     me = g * SUB + u
     y, zl, core, x, zh = g >> 2, (g >> 1) & 1, g & 1, u >> 1, u & 1
     z = zh * 2 + zl
-    par = zl ^ (x & 1) ^ (y & 1)
-    pm = (core << 6) | (par << 5) | (y << 3) | (x << 1) | zh
+    pm = (core << 6) | ((zl ^ (x & 1) ^ (y & 1)) << 5) | ((zh ^ (x >> 1) ^ (y >> 1)) << 4) | (y << 2) | x
     there = (x, y, z)
     axis1 = (x, y, z)
     index2 = (y * 4 + z, z * 4 + x, x * 4 + y)
@@ -137,29 +137,38 @@
     ).astype(BF)
     loads[4].wait()
 
-    others = remote(ix1.at[pl.ds(0, SUB - 1)], ix1.at[pl.ds(0, SUB - 1)], i1_s, i1_r, (g, u ^ 1))
-    others.wait_recv()
-
-    for r in range(8):
-        ixt[r] = jnp.concatenate([ix1[k, r : r + 1, :] for k in range(SUB)], axis=0)
-
-    def step2(o):
-        h = g ^ o
-        remote(ixt.at[h >> 1], ix2.at[g], i2_s, i2_r, (h, u)).start()
-
-    loop(1, GRP, step2)
-    ix2[g] = ixt[g >> 1]
-
     span = pl.ds(SMALL, (SUB - 1) * GIANT)
     rows_in = remote(etab.at[span], etab.at[span], gi_s, gi_r, (g, u ^ 1))
     rows_in.wait_recv()
     esend[...] = dot(one_t[...], etab[...], 0, 0).astype(BF).reshape(DEVICES, CAP, WIDTH)
 
+    others = remote(ix1.at[pl.ds(0, SUB - 1)], ix1.at[pl.ds(0, SUB - 1)], i1_s, i1_r, (g, u ^ 1))
+    others.wait_recv()
+
+    for r in range(8):
+        ixt[r] = jnp.concatenate([ix1[k, r : r + 1, :] for k in range(SUB)], axis=0)
+
+    def step2(o):
+        h = g ^ o
+        remote(ixt.at[h >> 1], ix2.at[g], i2_s, i2_r, (h, u)).start()
+
+    loop(1, GRP, step2)
+    ix2[g] = ixt[g >> 1]
+
+    def each_peer(c, step):
+        for i in range(1, PER):
+            step(c * PER + i)
+
+        if isinstance(c, int):
+            step(c * PER)
+        else:
+            pl.when(c > 0)(lambda: step(c * PER))
+
     def send_rows(s):
         j = me ^ mask_of(s)
-        remote(esend.at[j], erecv.at[pm], e_s, e_r.at[s >> 5], place(j)).start()
-
-    loop(1, DEVICES, send_rows)
+        remote(esend.at[j], erecv.at[pm], e_s, e_r.at[s // PER], place(j)).start()
+
+    loop(0, CHUNKS, lambda c: each_peer(c, send_rows))
     erecv[pm] = esend[me]
 
     half = ix2.at[pl.ds(0, GRP - 1)]
@@ -168,36 +177,23 @@
     table = ix2[...].reshape(DEVICES, 128)
     high, low = (table >> 8).astype(F32).astype(BF), (table & 255).astype(F32).astype(BF)
 
-    def source(q):
-        qy, qx = (q >> 3) & 3, (q >> 1) & 3
-        qz = ((q >> 5) & 1) ^ (qx & 1) ^ (qy & 1)
-        return (qy << 5) | (qz << 4) | (((q >> 6) & 1) << 3) | (qx << 1) | (q & 1)
-
     first = (me & 15) * CAP
     s_col = lax.broadcasted_iota(I32, (SLOTS, 128), 0)
     d_col = lax.broadcasted_iota(I32, (SLOTS, 128), 1)
-    pick = jnp.where(source(s_col >> 3) == d_col, 1.0, 0.0).astype(BF)
+    pick = jnp.where(mask_of(s_col >> 3) == d_col, 1.0, 0.0).astype(BF)
     values = dot(pick, high) * 256.0 + dot(pick, low)
     values = jnp.where(d_col == first + (s_col & 7), values, 0.0)
     col = jnp.sum(values, axis=1, keepdims=True).astype(I32)
     colb[...] = jnp.broadcast_to(col, (SLOTS, 128))
-    values = dot(high, pick, 0, 1) * 256.0 + dot(low, pick, 0, 1)
-    l_row = lax.broadcasted_iota(I32, (128, SLOTS), 0)
-    s_row = lax.broadcasted_iota(I32, (128, SLOTS), 1)
-    values = jnp.where(l_row == first + (s_row & 7), values, 0.0)
-    rowb[...] = jnp.sum(values, axis=0, keepdims=True).astype(I32)
-
     for load in loads[5:]:
         load.wait()
     gw[...] = jnp.zeros_like(gw)
     gb[...] = jnp.zeros_like(gb)
 
-    def chunk(c, last=False):
-        b = (pm >> 5) ^ c
-        rows = pl.ds(pl.multiple_of(b * ROWS, ROWS), ROWS)
-        blocks = pl.ds(pl.multiple_of(b * PER, PER), PER)
+    def gather(k):
+        rows = pl.ds(pl.multiple_of(k * 256, 256), 256)
         at = colb[rows]
-        lanes = lax.broadcasted_iota(I32, (ROWS, 128), 1)
+        lanes = lax.broadcasted_iota(I32, (256, 128), 1)
         hot = jnp.concatenate(
             [jnp.where(at == lanes + k * 128, 1.0, 0.0).astype(BF) for k in range(NODES // 128)],
             axis=1,
@@ -206,55 +202,58 @@
         og = dot(hot, ng[...]).astype(BF)
         nd_all[rows] = nd
         og_all[rows] = og
-        preact = dot(nd, win[pl.ds(0, WIDTH)]) + b_in[...]
-        hid_grad = dot(og, wout[...], 1, 1)
-
-        if last:
-            w = erecv.at[pl.ds(0, PER)]
-            remote(w, w, e_s, e_r.at[c], (g, u ^ 1)).wait_recv()
-        else:
-
-            @pl.when(c == 0)
-            def _():
-                w = erecv.at[pl.ds(0, PER - 1)]
-                remote(w, w, e_s, e_r.at[0], (g, u ^ 1)).wait_recv()
-
-            @pl.when(c > 0)
-            def _():
-                w = erecv.at[pl.ds(0, PER)]
-                remote(w, w, e_s, e_r.at[c], (g, u ^ 1)).wait_recv()
-
+        pre_n[rows] = dot(nd, win[pl.ds(0, WIDTH)]) + b_in[...]
+        hid_n[rows] = dot(og, wout[...], 1, 1)
+
+    gather(pm >> 5)
+
+    def arrive(c):
+        full = erecv.at[pl.ds(0, PER)]
+        part = erecv.at[pl.ds(0, PER - 1)]
+        if isinstance(c, int):
+            remote(full, full, e_s, e_r.at[c], (g, u ^ 1)).wait_recv()
+            return
+
+        @pl.when(c == 0)
+        def _():
+            remote(part, part, e_s, e_r.at[0], (g, u ^ 1)).wait_recv()
+
+        @pl.when(c > 0)
+        def _():
+            remote(full, full, e_s, e_r.at[c], (g, u ^ 1)).wait_recv()
+
+    def chunk(c, last=False):
+        b = (pm >> 4) ^ c
+        rows = pl.ds(pl.multiple_of(b * ROWS, ROWS), ROWS)
+        blocks = pl.ds(pl.multiple_of(b * PER, PER), PER)
+        arrive(c)
         er = erecv[blocks].reshape(ROWS, WIDTH)
-        preact = preact + dot(er, win[pl.ds(WIDTH, WIDTH)])
+        preact = pre_n[rows] + dot(er, win[pl.ds(WIDTH, WIDTH)])
         logistic = jax.nn.sigmoid(preact)
-        hidden = (preact * logistic).astype(BF)
-        pg = (hid_grad * logistic * (1.0 + preact * (1.0 - logistic))).astype(BF)
+        hid_all[rows] = (preact * logistic).astype(BF)
+        pg = (hid_n[rows] * logistic * (1.0 + preact * (1.0 - logistic))).astype(BF)
         pg_all[rows] = pg
-
-        def weights(k, left, right):
-            gw[pl.ds(k * WIDTH, WIDTH)] += dot(left, right, 0, 0)
+        gb[...] += jnp.sum(pg.astype(F32), axis=0, keepdims=True)
+        if not last:
+            terms(b)
+            send_terms(c)
+
+    def terms(b):
+        rows = pl.ds(pl.multiple_of(b * ROWS, ROWS), ROWS)
+        term = dot(pg_all[rows], win[pl.ds(WIDTH, WIDTH)], 1, 1).astype(BF)
+        tsend[pl.ds(pl.multiple_of(b * PER, PER), PER)] = term.reshape(PER, CAP, WIDTH)
+
+    def weights(k, last=False):
+        b = (pm >> 5) ^ k
+        rows = pl.ds(pl.multiple_of(b * 256, 256), 256)
+        er = erecv[pl.ds(pl.multiple_of(b * 32, 32), 32)].reshape(256, WIDTH)
+        for p, (left, right) in enumerate(((nd_all[rows], pg_all[rows]), (er, pg_all[rows]), (hid_all[rows], og_all[rows]))):
+            gw[pl.ds(p * WIDTH, WIDTH)] += dot(left, right, 0, 0)
             if last:
-                reduce0(k)
-
-        def terms():
-            term = dot(pg, win[pl.ds(WIDTH, WIDTH)], 1, 1).astype(BF)
-            tsend[blocks] = term.reshape(PER, CAP, WIDTH)
-
-        if not last:
-            terms()
-            send_terms(c)
-        weights(0, nd, pg)
-        weights(1, er, pg)
-        weights(2, hidden, og)
-        gb[...] += jnp.sum(pg.astype(F32), axis=0, keepdims=True)
-        if last:
-            terms()
+                reduce0(p)
 
     def send_terms(c):
-        def one(s):
-            remote(tsend.at[pm ^ s], trecv.at[me], t_s, t_r, place(me ^ mask_of(s))).start()
-
-        loop(c * PER + jnp.where(c == 0, 1, 0), (c + 1) * PER, one)
+        each_peer(c, lambda s: remote(tsend.at[pm ^ s], trecv.at[me], t_s, t_r, place(me ^ mask_of(s))).start())
 
     twin = (g ^ 1, u)
 
@@ -265,13 +264,29 @@
                 S[h, p, i] = gw[top : top + 256, left : left + 128].astype(BF)
         remote(S.at[1 - core, p], r0.at[p], w_s.at[0, p], w_r.at[0, p], twin).start()
 
-    loop(0, CHUNKS - 1, chunk)
+    def pair(k):
+        chunk(2 * k)
+        chunk(2 * k + 1)
+        gather((pm >> 5) ^ (k + 1))
+        weights(k)
+
+    loop(0, CHUNKS // 2 - 1, pair)
+    chunk(CHUNKS - 2)
     chunk(CHUNKS - 1, True)
+    terms((pm >> 4) ^ (CHUNKS - 1))
+    send_terms(CHUNKS - 1)
+    weights(CHUNKS // 2 - 1, True)
     trecv[me] = tsend[pm]
     for i in range(4):
         bb0[core, i : i + 1, :] = gb[:, 128 * i : 128 * i + 128]
     bias0 = remote(bb0.at[core], bb0.at[core], b_s.at[0], b_r.at[0], twin)
     bias0.start()
+
+    values = dot(high, pick, 0, 1) * 256.0 + dot(low, pick, 0, 1)
+    l_row = lax.broadcasted_iota(I32, (128, SLOTS), 0)
+    s_row = lax.broadcasted_iota(I32, (128, SLOTS), 1)
+    values = jnp.where(l_row == first + (s_row & 7), values, 0.0)
+    rowb[...] = jnp.sum(values, axis=0, keepdims=True).astype(I32)
 
     nt[...] = dot(pg_all[...], win[pl.ds(0, WIDTH)], 1, 1).astype(BF)
 
@@ -288,7 +303,6 @@
         waits.append(done)
 
     waits = [bias0]
-    send_terms(CHUNKS - 1)
     loop(0, 2, node_tile)
     for p in range(3):
         settle(r0.at[p], 0, p)
@@ -418,6 +432,7 @@
             V((SLOTS, 128), I32), V((1, SLOTS), I32),
             V(wide, BF), V(wide, BF), V(wide, BF), V(wide, BF),
             V((SLOTS, WIDTH), BF), V((SLOTS, WIDTH), BF), V((SLOTS, WIDTH), BF), V((SLOTS, WIDTH), BF),
+            V((SLOTS, WIDTH), BF), V((SLOTS, WIDTH), F32), V((SLOTS, WIDTH), F32),
             V((3 * WIDTH, WIDTH), F32), V((1, WIDTH), F32),
             V((2, 3, 4, 256, 128), BF), V((3, 4, 256, 128), BF),
             V((3, 4, 256, 128), BF), V((3, 4, 256, 128), BF),

time: 65.4 us -> 63.2 us (0.966)
  Pallas kernels: 64.6 us -> 62.5 us
    pallas_call x1, Pallas kernels: 62.1 us -> 60 us  [layer(): pl.pallas_call(layer_kernel, out_shape=(V((NODES, WIDTH), BF), V((SMALL,...]
where the time goes in v4:
time: 63.2 us; the launch traced here: 63.1 us
  Pallas kernels  62.5 us (99%)
  between operations  0.64 us (1%)
    pallas_call x1, Pallas kernels, layer(): pl.pallas_call(layer_kernel, out_shape=(V((NODES, WIDTH), BF), V((SMALL,...  60 us
    pallas_call x1, Pallas kernels, finish(): pl.pallas_call(finish_kernel, out_shape=(shape((NODES, WIDTH), BF), shape...  2.5 us

profile of v4, /device:TPU:1, one launch (start us, length us, event | category | flops | bytes accessed | tf_op | source)
XLA Modules:
  0.0 63.1 jit_solution(4881562860420564521)
XLA Ops:
  0.6 60.0 %layer.1 = (bf16[2048,512]{1,0:T(8,128)(2,1)S(1)}, bf16[256,512]{1,0:T(8,128)(2,1)S(1)}, bf16[16,512]{1,0:T(8,128)(2,1)S(1)}, f32[3,512,512]{2,1,0:T(8,128)S(1)}, f32[1,512]{1,0:T(1,128)S(1)}) custom-call(bf16[2048,512]{1,0:T(8,128)(2,1)} %nf_in.1, bf16[2048,512]{1,0:T(8,128)(2,1)} %ng_in.1, bf16[256,512]{1,0:T(8,128)(2,1)} %small_in.1, ...), custom_call_target="tpu_custom_call" | custom-call | tf_op jit(solution)/shard_map/layer/pallas_call | solution.py:417
  60.6 2.5 %finish.1 = (bf16[2048,512]{1,0:T(8,128)(2,1)}, bf16[256,512]{1,0:T(8,128)(2,1)}, bf16[16,512]{1,0:T(8,128)(2,1)}, f32[1024,512]{1,0:T(8,128)}, f32[1,512]{1,0:T(1,128)}, /*index=5*/f32[512,512]{1,0:T(8,128)}) custom-call(bf16[2048,512]{1,0:T(8,128)(2,1)S(1)} %get-tuple-element.17.nodes, bf16[256,512]{1,0:T(8,128)(2,1)S(1)} %get-tuple-element.18.small, ...), custom_call_target="tpu_custom_call" | custom-call | tf_op jit(solution)/shard_map/finish/pallas_call | solution.py:465
